TPU v7x, 512 devices: a whole 4x4x16 slice. The times are simulated.
512 devices in a mesh: pts: 64 (over z, x_hi, core), sub: 8 (over x_lo, y).
Axes of the slice: x: 4 (x_hi: 2, x_lo: 2; x = x_hi * 2 + x_lo), y: 4, z: 16, core: 2. Of those that a mesh axis runs over, the one named last changes fastest.
Arguments:
- points: bfloat16 [262144, 256], P(('pts', 'sub')), may hold values from -6 to 6
- counts: int32 [64, 8], P('pts', 'sub'), may hold values from 1 to 512, as said below
- norm_gain: float32 [256], replicated, may hold values from 0.25 to 1.75
- w_fx: bfloat16 [256, 256], replicated, may hold values from -0.375 to 0.375
- w_slice: bfloat16 [256, 512], replicated, may hold values from -0.375 to 0.375
- temper: float32 [8], replicated, may hold values from 0.03 to 0.6
- query_projection: float32 [8, 32, 32], replicated, may hold values from -1 to 1
- key_projection: float32 [8, 32, 32], replicated, may hold values from -1 to 1
- value_projection: float32 [8, 32, 32], replicated, may hold values from -1 to 1
- w_out: bfloat16 [256, 256], replicated, may hold values from -0.375 to 0.375
- cotangent: bfloat16 [262144, 256], P(('pts', 'sub')), may hold values from -6 to 6
Outputs:
- updated: bfloat16 [262144, 256], P(('pts', 'sub'))
- grad_points: bfloat16 [262144, 256], P(('pts', 'sub'))
Inputs may be any that keep to these rules, and one draw needn't show every extreme that they name: `counts`: partitions differ in load: a device's count lies near 512, 256 or 128, some device is full.
All inputs are finite; a program needn't handle non-finite values.
Results may differ from a plain program's by a relative error of at most 0.006.
Values sent between devices are 32-bit elements; how exact they have to be, the bound alone decides.
No kernel may reach another device: no remote copies, remote signals or barrier semaphores. Data moves between devices by JAX's collectives and lax.ppermute only.
A program may use at most 64 MiB of HBM per device.

v0:
```python
import jax
import jax.numpy as jnp
from jax import lax
from jax.sharding import PartitionSpec as P


def forward_parts(xf, live, norm_gain, w_fx, w_slice, temper):
    rows = xf.shape[0]
    heads = temper.shape[0]
    mean = jnp.mean(xf, -1, keepdims=True)
    cent = xf - mean
    var = jnp.mean(cent * cent, -1, keepdims=True)
    normed = (cent * lax.rsqrt(var + 1e-05) * norm_gain).astype(jnp.bfloat16)
    point_features = jnp.dot(normed, w_fx, preferred_element_type=jnp.float32).reshape(
        rows, heads, -1
    )
    logits = jnp.dot(normed, w_slice, preferred_element_type=jnp.float32).reshape(rows, heads, -1)
    slice_weights = jax.nn.softmax(logits / temper[None, :, None], axis=-1) * live[:, None, None]
    numerator_sum = jnp.einsum(
        "wba,wbz->baz", slice_weights, point_features, precision=lax.Precision.HIGHEST
    )
    den = jnp.sum(slice_weights, axis=0)
    return (numerator_sum, den, slice_weights)


def slice_attention(numerator_sum, den, query_projection, key_projection, value_projection):
    slice_tokens = numerator_sum / (den[..., None] + 1e-05)
    slice_query = jnp.einsum(
        "xlw,xwi->xli", slice_tokens, query_projection, precision=lax.Precision.HIGHEST
    )
    slice_keys = jnp.einsum(
        "xlw,xwi->xli", slice_tokens, key_projection, precision=lax.Precision.HIGHEST
    )
    slice_values = jnp.einsum(
        "xlw,xwi->xli", slice_tokens, value_projection, precision=lax.Precision.HIGHEST
    )
    scores = jnp.einsum(
        "hme,hne->hmn", slice_query, slice_keys, precision=lax.Precision.HIGHEST
    ) / jnp.sqrt(jnp.float32(slice_query.shape[-1]))
    probs = jax.nn.softmax(scores, axis=-1)
    return jnp.einsum("hmn,hne->hme", probs, slice_values, precision=lax.Precision.HIGHEST)


def deslice(xf, slice_weights, att, w_out):
    rows = xf.shape[0]
    mixed = jnp.einsum("rhm,hme->rhe", slice_weights, att, precision=lax.Precision.HIGHEST)
    mixed = mixed.reshape(rows, -1).astype(jnp.bfloat16)
    return xf + jnp.dot(mixed, w_out, preferred_element_type=jnp.float32)


def per_device(
    points,
    counts,
    norm_gain,
    w_fx,
    w_slice,
    temper,
    query_projection,
    key_projection,
    value_projection,
    w_out,
    cotangent,
):
    rows = points.shape[0]
    live = (jnp.arange(rows, dtype=jnp.int32) < counts[0, 0]).astype(jnp.float32)
    xf = points.astype(jnp.float32)

    def front(xv):
        return forward_parts(xv, live, norm_gain, w_fx, w_slice, temper)

    (num_part, den_part, slice_weights), pull_front = jax.vjp(front, xf)
    numerator_sum, den = lax.psum((num_part, den_part), ("pts", "sub"))

    def middle(num_in, den_in):
        return slice_attention(num_in, den_in, query_projection, key_projection, value_projection)

    att, pull_middle = jax.vjp(middle, numerator_sum, den)

    def back(xv, weights_in, att_in):
        return deslice(xv, weights_in, att_in, w_out)

    updated, pull_back = jax.vjp(back, xf, slice_weights, att)
    grad_direct, grad_weights, grad_att_part = pull_back(cotangent.astype(jnp.float32))
    grad_att = lax.psum(grad_att_part, ("pts", "sub"))
    grad_num, grad_den = pull_middle(grad_att)
    grad_front = pull_front((grad_num, grad_den, grad_weights))[0]
    grad = (grad_direct + grad_front).astype(jnp.bfloat16)
    return (updated.astype(jnp.bfloat16), grad)


def solution(mesh):
    return jax.shard_map(
        per_device,
        mesh=mesh,
        in_specs=(
            P(("pts", "sub"), None),
            P("pts", "sub"),
            P(),
            P(),
            P(),
            P(),
            P(),
            P(),
            P(),
            P(),
            P(("pts", "sub"), None),
        ),
        out_specs=(P(("pts", "sub"), None), P(("pts", "sub"), None)),
        check_vma=False,
    )
```

profile of v0, /device:TPU:1, one launch (start us, length us, event | category | flops | bytes accessed | tf_op | source)
XLA Modules:
  0.0 499.8 jit_solution(5162263994449293648)
XLA Ops:
  7.2 1.2 convert_reduce_fusion
  9.4 0.6 copy-done.10
  10.0 0.4 fusion.31
  10.7 0.5 fusion.40
  11.5 0.7 copy-done.2
  12.4 1.6 fusion.38
  14.0 2.0 fusion.39
  16.2 0.4 fusion.9
  16.6 111.7 %psum.22 = f32[8,64]{1,0:T(8,128)S(1)} all-reduce(f32[8,64]{1,0:T(8,128)S(1)} %reduce_sum.98), channel_id=1, replica_groups=mesh['pts'=64,'sub'=8] {'pts','sub'}, use_global_device_ids=true, to_apply=%region_6.0 | all-reduce | flops 512 | bytes 4096 | tf_op jit(solution)/shard_map/psum | solution.py:72
  128.3 349.5 %all-reduce.3.cloned.1.call-done = (f32[8,64,32]{1,2,0:T(8,128)}, f32[8,64,32]{1,2,0:T(8,128)}) async-done(((f32[8,64,32]{1,2,0:T(8,128)}, f32[8,64,32]{1,2,0:T(8,128)}), (f32[8,64,32]{1,2,0:T(8,128)}, f32[8,64,32]{1,2,0:T(8,128)})) %all-reduce.3.cloned.1.call-update) | async-done | bytes 131088 | tf_op jit(solution)/shard_map/psum | solution.py:72
  477.8 1.4 fusion.29
  479.2 0.4 fusion.30
  479.6 0.6 fusion.41
  480.4 0.8 copy-done.5
  481.2 0.4 fusion.28
  481.6 0.5 copy-done.6
  482.1 0.6 multiply_reduce_fusion.1
  482.7 0.4 fusion.35
  483.1 0.6 fusion.36
  483.7 0.5 fusion.21
  484.3 0.4 fusion.23
  485.2 0.3 multiply_reduce_fusion.2
  485.5 0.9 fusion.25
  486.4 0.9 convolution_convert_fusion.3
  487.4 0.6 fusion.2
  488.0 1.3 multiply_reduce_fusion
  489.3 0.4 multiply_divide_fusion
  489.7 0.4 fusion.43
  490.1 0.4 fusion.18
  490.5 0.4 fusion.37
  490.9 1.0 add_convert_fusion
  492.0 1.0 fusion.3
  (42 shorter events, 2.0 us)
Async XLA Ops:
  7.2 3.3 copy-start
  7.2 1.2 copy-start.1
  7.2 470.7 %all-reduce.3.cloned.1.call-start = ((), (), s32[]{:S(2)}) async-start(), calls=%async_computation | async-start | bytes 524288 | tf_op jit(solution)/shard_map/psum | solution.py:72
  8.4 0.9 copy-start.4
  9.3 0.7 copy-start.10
  10.0 0.7 copy-start.11
  11.2 1.0 copy-start.2
  11.2 1.0 copy-start.3
  16.2 461.7 %copy-start.7 = (f32[8,32,32]{2,1,0:T(8,128)S(1)}, f32[8,32,32]{2,1,0:T(8,128)}, u32[]{:S(2)}) copy-start(f32[8,32,32]{2,1,0:T(8,128)} %param.18) | copy-start | bytes 98308
  477.8 1.4 copy-start.8
  477.8 1.4 copy-start.9
  480.3 0.9 copy-start.5
  481.2 0.9 copy-start.6
Sparse Core Ops, SparseCore 0:
  16.1 461.6 all-reduce.2
where the time goes:
time: 500 us
  waiting for transfers between devices  350 us (70%)
  blocking collectives  112 us (22%)
  matrix products  16.4 us (3%)
  between operations  15 us (3%)
    psum x1, waiting for transfers between devices, per_device(): numerator_sum, den = lax.psum((num_part, den_part), ('pts', 'sub'))  350 us
    psum x1, blocking collectives, per_device(): numerator_sum, den = lax.psum((num_part, den_part), ('pts', 'sub'))  112 us
  transfers between devices with their start and end apart: 1, of which 1 were waited for; matrix products, arithmetic and copies ran while one was open for 0% of the time, Pallas kernels for 0%

commit v1 on v0

--- a/solution.py
+++ b/solution.py
@@ -1,7 +1,10 @@
 import jax
 import jax.numpy as jnp
 from jax import lax
-from jax.sharding import PartitionSpec as P
+from jax.sharding import Mesh, PartitionSpec as P
+
+PLANE = ("xh", "c", "xl", "y")
+ALL = ("z", "xh", "c", "xl", "y")
 
 
 def forward_parts(xf, live, norm_gain, w_fx, w_slice, temper):
@@ -48,6 +51,13 @@
     return xf + jnp.dot(mixed, w_out, preferred_element_type=jnp.float32)
 
 
+def sum_all(flat):
+    part = lax.all_to_all(flat.reshape(32, 9, 1, 128), PLANE, 0, 0).sum(0)
+    part = lax.all_to_all(jnp.broadcast_to(part[None], (16, 9, 1, 128)), "z", 0, 0).sum(0)
+    whole = lax.all_to_all(jnp.broadcast_to(part[None], (32, 9, 1, 128)), PLANE, 0, 0)
+    return whole.reshape(288, 128)
+
+
 def per_device(
     points,
     counts,
@@ -69,19 +79,36 @@
         return forward_parts(xv, live, norm_gain, w_fx, w_slice, temper)
 
     (num_part, den_part, slice_weights), pull_front = jax.vjp(front, xf)
-    numerator_sum, den = lax.psum((num_part, den_part), ("pts", "sub"))
+
+    def back(xv, weights_in, att_in):
+        return deslice(xv, weights_in, att_in, w_out)
+
+    gmixed = jnp.dot(cotangent, w_out.T, preferred_element_type=jnp.float32).astype(jnp.bfloat16)
+    gatt_part = jnp.einsum(
+        "rhm,rhe->hme",
+        slice_weights,
+        gmixed.astype(jnp.float32).reshape(rows, 8, 32),
+        precision=lax.Precision.HIGHEST,
+    )
+    flat = jnp.concatenate(
+        [
+            num_part.reshape(128, 128),
+            gatt_part.reshape(128, 128),
+            den_part.reshape(4, 128),
+            jnp.zeros((28, 128), jnp.float32),
+        ]
+    )
+    flat = sum_all(flat)
+    numerator_sum = flat[:128].reshape(8, 64, 32)
+    grad_att = flat[128:256].reshape(8, 64, 32)
+    den = flat[256:260].reshape(8, 64)
 
     def middle(num_in, den_in):
         return slice_attention(num_in, den_in, query_projection, key_projection, value_projection)
 
     att, pull_middle = jax.vjp(middle, numerator_sum, den)
-
-    def back(xv, weights_in, att_in):
-        return deslice(xv, weights_in, att_in, w_out)
-
     updated, pull_back = jax.vjp(back, xf, slice_weights, att)
-    grad_direct, grad_weights, grad_att_part = pull_back(cotangent.astype(jnp.float32))
-    grad_att = lax.psum(grad_att_part, ("pts", "sub"))
+    grad_direct, grad_weights, _ = pull_back(cotangent.astype(jnp.float32))
     grad_num, grad_den = pull_middle(grad_att)
     grad_front = pull_front((grad_num, grad_den, grad_weights))[0]
     grad = (grad_direct + grad_front).astype(jnp.bfloat16)
@@ -89,22 +116,12 @@
 
 
 def solution(mesh):
+    fine = Mesh(mesh.devices.reshape(16, 2, 2, 2, 4), ALL)
+    rows = P(ALL, None)
     return jax.shard_map(
         per_device,
-        mesh=mesh,
-        in_specs=(
-            P(("pts", "sub"), None),
-            P("pts", "sub"),
-            P(),
-            P(),
-            P(),
-            P(),
-            P(),
-            P(),
-            P(),
-            P(),
-            P(("pts", "sub"), None),
-        ),
-        out_specs=(P(("pts", "sub"), None), P(("pts", "sub"), None)),
+        mesh=fine,
+        in_specs=(rows, P(("z", "xh", "c"), ("xl", "y"))) + (P(),) * 8 + (rows,),
+        out_specs=(rows, rows),
         check_vma=False,
     )

time: 500 us -> 91.4 us (0.18)
  waiting for transfers between devices: 350 us -> 7.24 us
  blocking collectives: 112 us -> 42.6 us
  between operations: 15 us -> 1.79 us
  local copies, waits for them, and re-layouts: 3.16 us -> 12.4 us
  starting transfers between devices: 0.04 us -> 5.59 us
    psum x1 -> x0, waiting for transfers between devices: 350 us -> none  [per_device(): numerator_sum, den = lax.psum((num_part, den_part), ('pts', 'sub'))]
    psum x1 -> x0, blocking collectives: 112 us -> none  [per_device(): numerator_sum, den = lax.psum((num_part, den_part), ('pts', 'sub'))]
    all_to_all x0 -> x2, blocking collectives: none -> 42.6 us  [the longest x1 25.2 us: sum_all(): lax.all_to_all(jnp.broadcast_to(part[None], (16, 9, 1, 128)), 'z', 0, 0)]
    all_to_all x0 -> x1, waiting for transfers between devices: none -> 7.24 us  [sum_all(): lax.all_to_all(jnp.broadcast_to(part[None], (32, 9, 1, 128)), PLANE, 0, 0)]
    unnamed x24 -> x74, local copies, waits for them, and re-layouts: 2.94 us -> 9.25 us
    all_to_all x0 -> x1, starting transfers between devices: none -> 5.59 us  [sum_all(): lax.all_to_all(jnp.broadcast_to(part[None], (32, 9, 1, 128)), PLANE, 0, 0)]
  transfers between devices with their start and end apart: 1 -> 1, of which waited for: 1 -> 1; matrix products, arithmetic and copies ran while one was open for 0% -> 1% of each run, Pallas kernels for 0% -> 0%
where the time goes in v1:
time: 91.4 us; the launch traced here: 90.7 us
  blocking collectives  42.6 us (47%)
  matrix products  15.6 us (17%)
  local copies, waits for them, and re-layouts  12.4 us (14%)
  waiting for transfers between devices  7.24 us (8%)
  starting transfers between devices  5.59 us (6%)
  other arithmetic  5.44 us (6%)
  between operations  1.79 us (2%)
    all_to_all x1, blocking collectives, sum_all(): lax.all_to_all(jnp.broadcast_to(part[None], (16, 9, 1, 128)), 'z', 0, 0)  25.2 us
    all_to_all x1, blocking collectives, sum_all(): part = lax.all_to_all(flat.reshape(32, 9, 1, 128), PLANE, 0, 0).sum(0)  17.4 us
    unnamed x74, local copies, waits for them, and re-layouts  9.25 us
    all_to_all x1, waiting for transfers between devices, sum_all(): lax.all_to_all(jnp.broadcast_to(part[None], (32, 9, 1, 128)), PLANE, 0, 0)  7.24 us
    all_to_all x1, starting transfers between devices, sum_all(): lax.all_to_all(jnp.broadcast_to(part[None], (32, 9, 1, 128)), PLANE, 0, 0)  5.59 us
    dot_general x3, matrix products, forward_parts(): jnp.einsum('wba,wbz->baz', slice_weights, point_features, precision=lax.P...  3.55 us
    dot_general x3, matrix products, slice_attention(): jnp.einsum('hmn,hne->hme', probs, slice_values, precision=lax.Precision.H...  2.55 us
  transfers between devices with their start and end apart: 1, of which 1 were waited for; matrix products, arithmetic and copies ran while one was open for 1% of the time, Pallas kernels for 0%

profile of v1, /device:TPU:1, one launch (start us, length us, event | category | flops | bytes accessed | tf_op | source)
XLA Modules:
  0.0 90.7 jit_solution(1790976395532360511)
XLA Ops:
  0.7 1.2 %convert_reduce_fusion = f32[512]{0:T(512)S(1)} fusion(bf16[512,256]{1,0:T(8,128)(2,1)} %param.11), kind=kLoop, calls=%fused_computation.28 | loop fusion | flops 261632 | bytes 264192 | tf_op jit(solution)/shard_map/jvp()/reduce_sum | solution.py:13
  2.1 0.6 copy-done.24
  3.4 0.6 copy-done.31
  5.5 1.3 %fusion.39 = f32[8,64,32]{2,1,0:T(8,128)S(1)} fusion(f32[512,8,32]{0,2,1:T(8,128)S(1)} %bitcast.86, f32[512]{0:T(512)S(1)} %fusion.26, f32[512,8]{0,1:T(8,128)S(1)} %fusion.14, f32[512,8]{0,1:T(8,128)S(1)} %get-tuple-element.4, f32[512,8,64]{0,2,1:T(8,128)S(1)} %bitcast.76, f32[8]{0:T(128)S(1)} %copy-done.33), kind=kOutput, calls=%fused_computation.72 | convolution fusion | flops 101711872 | bytes 1673248 | tf_op jit(solution)/shard_map/jvp(wba,wbz->baz)/dot_general | solution.py:22
  6.9 0.8 copy-done.2
  8.0 0.9 fusion.38
  9.7 17.4 %all_to_all.15 = f32[32,9,1,128]{3,2,1,0:T(1,128)S(1)} all-to-all(f32[32,9,1,128]{3,2,1,0:T(1,128)S(1)} %bitcast.83), channel_id=1, replica_groups=mesh['z'=16,'xh'=2,'c'=2,'xl'=2,'y'=4] {'xh','c','xl','y'}, dimensions={0} | all-to-all | bytes 294912 | tf_op jit(solution)/shard_map/all_to_all | solution.py:55
  27.3 25.2 %all_to_all.16 = f32[16,9,1,128]{3,2,1,0:T(1,128)S(1)} all-to-all(f32[16,9,1,128]{3,2,1,0:T(1,128)S(1)} %broadcast_in_dim.19), channel_id=1, replica_groups=mesh['z'=16,'xh'=2,'c'=2,'xl'=2,'y'=4] {'z'}, dimensions={0} | all-to-all | bytes 147456 | tf_op jit(solution)/shard_map/all_to_all | solution.py:56
  52.6 0.7 broadcast_in_dim.20
  53.3 5.6 %all-to-all-start.2 = ((f32[32,9,1,128]{3,2,1,0:T(1,128)}), f32[32,9,1,128]{3,2,1,0:T(1,128)S(1)}, u32[]{:S(2)}, u32[]{:S(2)}) async-start(f32[32,9,1,128]{3,2,1,0:T(1,128)} %broadcast_in_dim.20), calls=%async_computation.2 | async-start | bytes 294912 | tf_op jit(solution)/shard_map/all_to_all | solution.py:57
  58.9 0.6 multiply_divide_fusion.1
  59.5 7.2 %all-to-all-done.2 = f32[32,9,1,128]{3,2,1,0:T(1,128)S(1)} async-done(((f32[32,9,1,128]{3,2,1,0:T(1,128)}), f32[32,9,1,128]{3,2,1,0:T(1,128)S(1)}, u32[]{:S(2)}, u32[]{:S(2)}) %all-to-all-start.2) | async-done | bytes 147488 | tf_op jit(solution)/shard_map/all_to_all | solution.py:57
  66.8 0.6 fusion.41
  67.8 0.7 copy-done.10
  68.8 0.5 copy-done.12
  70.0 0.6 fusion.42
  70.8 0.5 copy-done.22
  71.3 0.6 multiply_divide_fusion.3
  71.9 1.0 %fusion.28 = f32[8,64,32]{1,2,0:T(8,128)} fusion(f32[8,32,32]{2,1,0:T(8,128)S(1)} %copy-done.7, f32[8,64,32]{1,2,0:T(8,128)S(1)} %copy.66, f32[8,64]{1,0:T(8,128)S(1)} %add.40), kind=kOutput, calls=%fused_computation.63 | convolution fusion | flops 6307840 | bytes 165888 | tf_op jit(solution)/shard_map/jvp(xlw,xwi->xli)/dot_general | solution.py:37
  72.9 0.9 %reshape.142 = f32[8,64,32]{2,1,0:T(8,128)S(1)} reshape(f32[128,128]{1,0:T(8,128)} %get-tuple-element.2) | data formatting | bytes 131072 | tf_op jit(solution)/shard_map/reshape | solution.py:103
  73.9 1.6 %multiply_reduce_fusion.1 = (f32[8,64]{1,0:T(8,128)S(1)}, f32[8,64,64]{1,2,0:T(8,128)S(1)}) fusion(f32[8,64,64]{1,2,0:T(8,128)S(1)} %get-tuple-element.7, f32[8,64]{1,0:T(8,128)} %multiply_divide_fusion.3, f32[8,64]{1,0:T(8,128)} %copy-done.22, f32[8,64,32]{2,1,0:T(8,128)S(1)} %reshape.142, f32[8,64,32]{1,2,0:T(8,128)} %fusion.28), kind=kOutput, calls=%fused_computation.41 | convolution fusion | flops 12713472 | bytes 399360 | tf_op jit(solution)/shard_map/transpose(jvp(hmn,hne->hme))/dot_general | solution.py:44
  75.5 0.6 copy-done.23
  77.1 0.6 fusion.36
  77.7 0.6 fusion.21
  79.8 0.6 copy-done.11
  80.7 0.6 copy-done.13
  82.3 0.9 %fusion.25 = bf16[8,32,512]{2,1,0:T(8,128)(2,1)S(1)} fusion(f32[8,64,32]{1,2,0:T(8,128)S(1)} %get-tuple-element.11, f32[8,64]{1,0:T(8,128)S(1)} %copy-done.30, f32[512]{0:T(512)S(1)} %copy-done.36, f32[512,8]{0,1:T(8,128)S(1)} %copy-done.6, f32[512,8]{0,1:T(8,128)S(1)} %get-tuple-element.4, f32[512,8,64]{0,2,1:T(8,128)S(1)} %bitcast.78, f32[8]{0:T(128)S(1)} %copy-done.34), kind=kOutput, calls=%fused_computation.51 | convolution fusion | flops 101728256 | bytes 1413152 | tf_op jit(solution)/shard_map/transpose(jvp(wba,wbz->baz))/dot_general | solution.py:22
  83.2 0.9 %convolution_convert_fusion.2 = bf16[8,32,512]{2,1,0:T(8,128)(2,1)S(1)} fusion(f32[8,64,32]{1,2,0:T(8,128)S(1)} %fusion.23, f32[512]{0:T(512)S(1)} %copy-done.36, f32[512,8]{0,1:T(8,128)S(1)} %copy-done.6, f32[512,8]{0,1:T(8,128)S(1)} %get-tuple-element.4, f32[512,8,64]{0,2,1:T(8,128)S(1)} %bitcast.79, f32[8]{0:T(128)S(1)} %copy-done.34), kind=kOutput, calls=%fused_computation.8 | convolution fusion | flops 101842944 | bytes 1411104 | tf_op jit(solution)/shard_map/jvp(rhm,hme->rhe)/dot_general | solution.py:49
  84.1 0.6 fusion.2
  84.9 1.3 %multiply_reduce_fusion = (f32[512,8]{0,1:T(8,128)S(1)}, f32[512,8,64]{0,2,1:T(8,128)S(1)}) fusion(f32[512,8]{0,1:T(8,128)S(1)} %copy-done.28, f32[512,8]{0,1:T(8,128)S(1)} %get-tuple-element.4, f32[8]{0:T(128)S(1)} %copy-done.34, f32[512,512]{0,1:T(8,128)S(1)} %get-tuple-element.5, f32[512]{0:T(512)S(1)} %copy-done.36, f32[512,8,64]{0,2,1:T(8,128)S(1)} %fusion.2, ...), kind=kOutput, calls=%fused_computation.22 | convolution fusion | flops 102510592 | bytes 3788832 | tf_op jit(solution)/shard_map/transpose(jvp(wba,wbz->baz))/dot_general | solution.py:22
  88.7 1.1 %add_convert_fusion = bf16[512,256]{1,0:T(8,128)(2,1)} fusion(bf16[512,256]{1,0:T(8,128)(2,1)S(1)} %copy-done.2, f32[512]{0:T(512)S(1)} %negate_multiply_fusion, f32[512]{0:T(512)S(1)} %multiply_multiply_fusion.1, f32[512]{0:T(512)S(1)} %copy-done.19, bf16[512,256]{1,0:T(8,128)(2,1)S(1)} %copy-done.1, f32[512,256]{1,0:T(8,128)S(1)} %get-tuple-element.15, ...), kind=kLoop, calls=%fused_computation.38 | loop fusion | flops 1310720 | bytes 1318912 | tf_op jit(solution)/shard_map/convert_element_type | solution.py:114
  89.7 1.0 %fusion.3 = bf16[512,256]{1,0:T(8,128)(2,1)} fusion(bf16[512,256]{0,1:T(8,128)(2,1)S(1)} %bitcast.88, bf16[256,256]{1,0:T(8,128)(2,1)S(1)} %copy-done.3, bf16[512,256]{1,0:T(8,128)(2,1)S(1)} %copy-done.1), kind=kOutput, calls=%fused_computation.10 | convolution fusion | flops 67502080 | bytes 917504 | tf_op jit(solution)/shard_map/jvp()/dot_general | solution.py:51
  (106 shorter events, 10.7 us)
Async XLA Ops:
  0.6 3.8 %copy-start = (bf16[256,512]{1,0:T(8,128)(2,1)S(1)}, bf16[256,512]{1,0:T(8,128)(2,1)}, u32[]{:S(2)}) copy-start(bf16[256,512]{1,0:T(8,128)(2,1)} %param.15) | copy-start | bytes 786436
  0.6 1.2 %copy-start.1 = (bf16[512,256]{1,0:T(8,128)(2,1)S(1)}, bf16[512,256]{1,0:T(8,128)(2,1)}, u32[]{:S(2)}) copy-start(bf16[512,256]{1,0:T(8,128)(2,1)} %param.11) | copy-start | bytes 786436
  1.8 2.6 %copy-start.18 = (f32[512]{0:T(512)}, f32[512]{0:T(512)S(1)}, u32[]{:S(2)}) copy-start(f32[512]{0:T(512)S(1)} %broadcast_multiply_fusion) | copy-start | bytes 6148
  1.8 1.5 %copy-start.4 = (bf16[256,256]{1,0:T(8,128)(2,1)S(1)}, bf16[256,256]{1,0:T(8,128)(2,1)}, u32[]{:S(2)}) copy-start(bf16[256,256]{1,0:T(8,128)(2,1)} %param.14) | copy-start | bytes 393220
  2.7 1.8 %copy-start.20 = (f32[512]{0:T(512)}, f32[512]{0:T(512)S(1)}, u32[]{:S(2)}) copy-start(f32[512]{0:T(512)S(1)} %fusion.27) | copy-start | bytes 6148
  3.3 0.7 copy-start.31
  4.0 5.1 %copy-start.35 = (f32[512]{0:T(512)}, f32[512]{0:T(512)S(1)}, u32[]{:S(2)}) copy-start(f32[512]{0:T(512)S(1)} %fusion.26) | copy-start | bytes 6148
  5.5 53.5 %copy-start.5 = (f32[512,8]{0,1:T(8,128)}, f32[512,8]{0,1:T(8,128)S(1)}, u32[]{:S(2)}) copy-start(f32[512,8]{0,1:T(8,128)S(1)} %fusion.14) | copy-start | bytes 49156
  5.5 1.5 %copy-start.3 = (bf16[256,256]{1,0:T(8,128)(2,1)S(1)}, bf16[256,256]{1,0:T(8,128)(2,1)}, u32[]{:S(2)}) copy-start(bf16[256,256]{1,0:T(8,128)(2,1)} %param.20) | copy-start | bytes 393220
  6.8 1.0 %copy-start.2 = (bf16[512,256]{1,0:T(8,128)(2,1)S(1)}, bf16[512,256]{1,0:T(8,128)(2,1)}, u32[]{:S(2)}) copy-start(bf16[512,256]{1,0:T(8,128)(2,1)} %param.21) | copy-start | bytes 786436
  53.3 13.5 %all-to-all-start.2 = ((f32[32,9,1,128]{3,2,1,0:T(1,128)}), f32[32,9,1,128]{3,2,1,0:T(1,128)S(1)}, u32[]{:S(2)}, u32[]{:S(2)}) async-start(f32[32,9,1,128]{3,2,1,0:T(1,128)} %broadcast_in_dim.20), calls=%async_computation.2 | async-start | bytes 294912 | tf_op jit(solution)/shard_map/all_to_all | solution.py:57
  67.5 0.9 %copy-start.10 = (f32[8,32,32]{2,1,0:T(8,128)S(1)}, f32[8,32,32]{2,1,0:T(8,128)}, u32[]{:S(2)}) copy-start(f32[8,32,32]{2,1,0:T(8,128)} %param.18) | copy-start | bytes 98308
  68.5 3.4 %copy-start.29 = (f32[8,64]{1,0:T(8,128)}, f32[8,64]{1,0:T(8,128)S(1)}, u32[]{:S(2)}) copy-start(f32[8,64]{1,0:T(8,128)S(1)} %add.40) | copy-start | bytes 6148
  68.5 0.9 %copy-start.12 = (f32[8,32,32]{2,1,0:T(8,128)S(1)}, f32[8,32,32]{2,1,0:T(8,128)}, u32[]{:S(2)}) copy-start(f32[8,32,32]{2,1,0:T(8,128)} %param.17) | copy-start | bytes 98308
  70.7 1.2 %copy-start.7 = (f32[8,32,32]{2,1,0:T(8,128)S(1)}, f32[8,32,32]{2,1,0:T(8,128)}, u32[]{:S(2)}) copy-start(f32[8,32,32]{2,1,0:T(8,128)} %param.19) | copy-start | bytes 98308
  71.3 1.6 %copy-start.26 = (f32[8,64]{1,0:T(8,128)}, f32[8,64]{1,0:T(8,128)S(1)}, u32[]{:S(2)}) copy-start(f32[8,64]{1,0:T(8,128)S(1)} %fusion.20) | copy-start | bytes 6148
  73.9 1.6 %copy-start.17 = (f32[8,64,32]{1,2,0:T(8,128)S(1)}, f32[8,64,32]{1,2,0:T(8,128)}, u32[]{:S(2)}) copy-start(f32[8,64,32]{1,2,0:T(8,128)} %copy-done.16) | copy-start | bytes 196612
  75.5 0.7 copy-start.23
  75.5 0.7 copy-start.27
  76.2 0.9 copy-start.15
  77.7 0.7 copy-start.30
  77.7 0.9 %copy-start.9 = (f32[8,64,32]{1,2,0:T(8,128)S(1)}, f32[8,64,32]{1,2,0:T(8,128)}, u32[]{:S(2)}) copy-start(f32[8,64,32]{1,2,0:T(8,128)} %fusion.28) | copy-start | bytes 196612
  78.6 0.9 copy-start.8
  79.5 0.9 copy-start.11
  80.4 0.9 copy-start.13
  81.3 0.7 copy-start.6
  81.3 0.7 copy-start.36
  84.1 0.7 copy-start.28
  86.6 0.7 copy-start.19
  86.9 0.7 copy-start.32
  87.6 0.7 copy-start.25
  87.6 0.7 copy-start.21
  (6 other events, 3.8 us)

commit v2 on v1

v2 whole, which is shorter than its diff:
```python
import math

import jax
import jax.numpy as jnp
from jax import lax
from jax.experimental import pallas as pl
from jax.experimental.pallas import tpu as pltpu
from jax.sharding import Mesh, PartitionSpec as P

PLANE = ("xh", "c", "xl", "y")
ALL = ("z", "xh", "c", "xl", "y")
HEADS, SLICES, DH = 8, 64, 32
F32, BF16 = jnp.float32, jnp.bfloat16


def dot(a, b, ca, cb, precision=None):
    return lax.dot_general(
        a, b, (((ca,), (cb,)), ((), ())), precision=precision, preferred_element_type=F32
    )


def exact(a, b, ca, cb):
    return dot(a, b, ca, cb, lax.Precision.HIGHEST)


def normalise(x):
    cent = x - jnp.mean(x, -1, keepdims=True)
    rstd = lax.rsqrt(jnp.mean(cent * cent, -1, keepdims=True) + 1e-05)
    return cent * rstd, rstd


def front_kernel(
    count, temper, x_ref, gain, w_fx, w_slice, w_out, cot, flat, w_t, c_t, logit_t, w_bf
):
    rows = x_ref.shape[0]
    normed = (normalise(x_ref[...].astype(F32))[0] * gain[...]).astype(BF16)
    logit_t[...] = dot(w_slice[...].T, normed, 1, 1)
    feats = dot(w_fx[...].T, normed, 1, 1).astype(BF16)
    gmix = dot(w_out[...], cot[...], 1, 1).astype(BF16)
    for h in range(HEADS):
        c_t[h * 64 : h * 64 + 32, :] = feats[h * 32 : h * 32 + 32, :]
        c_t[h * 64 + 32 : h * 64 + 64, :] = gmix[h * 32 : h * 32 + 32, :]
    live = (lax.broadcasted_iota(jnp.int32, (1, rows), 1) < count[0, 0]).astype(F32)
    for h in range(HEADS):
        part = slice(h * SLICES, (h + 1) * SLICES)
        logits = logit_t[part, :]
        scale = 1.0 / jnp.full((1, rows), temper[h], F32)
        e = jnp.exp((logits - jnp.max(logits, 0, keepdims=True)) * scale)
        w = e * (live / jnp.sum(e, 0, keepdims=True))
        w_t[part, :] = w
        w_bf[part, :] = w.astype(BF16)
    lane = lax.broadcasted_iota(jnp.int32, (64, 128), 1)
    for p in range(4):
        part = slice(p * 128, (p + 1) * 128)
        both = dot(w_bf[part, :], c_t[part, :], 1, 1)
        flat[p * 64 : (p + 1) * 64, :] = jnp.where(lane < 64, both[:64], both[64:])
    den = dot(jnp.ones((8, rows), BF16), w_bf[...], 1, 1)
    flat[256:288, :] = jnp.zeros((32, 128), F32)
    for p in range(4):
        flat[256 + p : 257 + p, :] = den[0:1, p * 128 : (p + 1) * 128]


def middle(flat, query, key, value, b_hi, b_lo, gden):
    den_cols = flat[256:264, :].T
    own = (
        lax.broadcasted_iota(jnp.int32, (128, 128), 0) // 64
        == lax.broadcasted_iota(jnp.int32, (128, 128), 1) // 64
    )
    for p in range(4):
        heads = (2 * p, 2 * p + 1)
        t = flat[p * 64 : (p + 1) * 64, :]
        rec = 1.0 / (den_cols[:, p : p + 1] + 1e-05)
        tok = jnp.concatenate([t[:, 0:32], t[:, 64:96]], 0) * rec
        g_att = jnp.concatenate([t[:, 32:64], t[:, 96:128]], 0)

        def project(a, weights, side):
            return jnp.concatenate(
                [exact(a[i * 64 : (i + 1) * 64], weights[h], 1, side) for i, h in enumerate(heads)],
                0,
            )

        q, k, v = project(tok, query, 0), project(tok, key, 0), project(tok, value, 0)
        scale = 1.0 / math.sqrt(DH)
        s = jnp.where(own, exact(q, k, 1, 1) * scale, -jnp.inf)
        e = jnp.exp(s - jnp.max(s, -1, keepdims=True))
        prob = e / jnp.sum(e, -1, keepdims=True)
        att = exact(prob, v, 1, 0)
        g_v = exact(prob, g_att, 0, 0)
        g_prob = exact(g_att, v, 1, 1)
        g_s = prob * (g_prob - jnp.sum(prob * g_prob, -1, keepdims=True)) * scale
        g_q, g_k = exact(g_s, k, 1, 0), exact(g_s, q, 0, 0)
        g_tok = project(g_q, query, 1) + project(g_k, key, 1) + project(g_v, value, 1)
        g_num = g_tok * rec
        gden[p * 128 : (p + 1) * 128, :] = -jnp.sum(tok * g_num, -1, keepdims=True)
        block = jnp.concatenate([g_num, att], 1)
        block = jnp.where(own, jnp.concatenate([block, block], 1), 0.0)
        hi = block.astype(BF16)
        b_hi[p * 128 : (p + 1) * 128, :] = hi
        b_lo[p * 128 : (p + 1) * 128, :] = (block - hi.astype(F32)).astype(BF16)


def back_kernel(
    temper, flat, query, key, value, x_ref, gain, w_fx, w_slice, w_out, cot, w_t, c_t,
    updated, grad, b_hi, b_lo, gden, g_logit, g_feat, mixed_t,
):
    rows = x_ref.shape[0]
    middle(flat, query, key, value, b_hi, b_lo, gden)
    for p in range(4):
        part = slice(p * 128, (p + 1) * 128)
        w = w_t[part, :]
        both = dot(b_hi[part, :], w.astype(BF16), 0, 0)
        c = c_t[part, :]
        g_w = dot(b_hi[part, :], c, 1, 0) + dot(b_lo[part, :], c, 1, 0) + gden[part, :]
        for i in range(2):
            h = 2 * p + i
            g_feat[h * 32 : (h + 1) * 32, :] = both[i * 64 : i * 64 + 32].astype(BF16)
            mixed_t[h * 32 : (h + 1) * 32, :] = both[i * 64 + 32 : i * 64 + 64]
            mine = slice(i * 64, (i + 1) * 64)
            scale = 1.0 / jnp.full((1, rows), temper[h], F32)
            wh, gh = w[mine], g_w[mine]
            mean = jnp.sum(wh * gh, 0, keepdims=True)
            g_logit[h * 64 : (h + 1) * 64, :] = (wh * (gh - mean) * scale).astype(BF16)
    x = x_ref[...].astype(F32)
    mixed = mixed_t[...].T.astype(BF16)
    updated[...] = (x + dot(mixed, w_out[...], 1, 0)).astype(BF16)
    g_normed = dot(w_slice[...], g_logit[...], 1, 0) + dot(w_fx[...], g_feat[...], 1, 0)
    g_normed = g_normed.T.astype(BF16).astype(F32)
    xhat, rstd = normalise(x)
    g_hat = g_normed * gain[...]
    along = jnp.mean(g_hat * xhat, -1, keepdims=True)
    g_x = rstd * (g_hat - jnp.mean(g_hat, -1, keepdims=True) - xhat * along)
    grad[...] = (cot[...].astype(F32) + g_x).astype(BF16)


def sum_all(flat):
    part = lax.all_to_all(flat.reshape(32, 9, 1, 128), PLANE, 0, 0).sum(0)
    part = lax.all_to_all(jnp.broadcast_to(part[None], (16, 9, 1, 128)), "z", 0, 0).sum(0)
    whole = lax.all_to_all(jnp.broadcast_to(part[None], (32, 9, 1, 128)), PLANE, 0, 0)
    return whole.reshape(288, 128)


VMEM = pl.BlockSpec(memory_space=pltpu.VMEM)
SMEM = pl.BlockSpec(memory_space=pltpu.SMEM)
PARAMS = pltpu.CompilerParams(vmem_limit_bytes=32 * 1024 * 1024)


def per_device(
    points,
    counts,
    norm_gain,
    w_fx,
    w_slice,
    temper,
    query_projection,
    key_projection,
    value_projection,
    w_out,
    cotangent,
):
    rows, width = points.shape
    gain = norm_gain.reshape(1, width)
    n = HEADS * SLICES
    flat, w_t, c_t = pl.pallas_call(
        front_kernel,
        out_shape=(
            jax.ShapeDtypeStruct((288, 128), F32),
            jax.ShapeDtypeStruct((n, rows), F32),
            jax.ShapeDtypeStruct((n, rows), BF16),
        ),
        in_specs=[SMEM] * 2 + [VMEM] * 6,
        out_specs=(VMEM,) * 3,
        scratch_shapes=[pltpu.VMEM((n, rows), F32), pltpu.VMEM((n, rows), BF16)],
        compiler_params=PARAMS,
        name="front",
    )(counts, temper, points, gain, w_fx, w_slice, w_out, cotangent)
    flat = sum_all(flat)
    return pl.pallas_call(
        back_kernel,
        out_shape=(jax.ShapeDtypeStruct((rows, width), BF16),) * 2,
        in_specs=[SMEM] + [VMEM] * 12,
        out_specs=(VMEM,) * 2,
        scratch_shapes=[
            pltpu.VMEM((n, 128), BF16),
            pltpu.VMEM((n, 128), BF16),
            pltpu.VMEM((n, 1), F32),
            pltpu.VMEM((n, rows), BF16),
            pltpu.VMEM((width, rows), BF16),
            pltpu.VMEM((width, rows), F32),
        ],
        compiler_params=PARAMS,
        name="back",
    )(
        temper, flat, query_projection, key_projection, value_projection, points, gain, w_fx,
        w_slice, w_out, cotangent, w_t, c_t,
    )


def solution(mesh):
    fine = Mesh(mesh.devices.reshape(16, 2, 2, 2, 4), ALL)
    rows = P(ALL, None)
    return jax.shard_map(
        per_device,
        mesh=fine,
        in_specs=(rows, P(("z", "xh", "c"), ("xl", "y"))) + (P(),) * 8 + (rows,),
        out_specs=(rows, rows),
        check_vma=False,
    )
```

time: 91.4 us -> 73.2 us (0.80)
  matrix products: 15.6 us -> 0 us
  blocking collectives: 42.6 us -> 56 us
  Pallas kernels: 0 us -> 9.87 us
  waiting for transfers between devices: 7.24 us -> 0 us
  local copies, waits for them, and re-layouts: 12.4 us -> 5.47 us
  starting transfers between devices: 5.59 us -> 0 us
  other arithmetic: 5.44 us -> 0.16 us
    dot_general x24 -> x0, matrix products: 15.6 us -> none  [the longest x3 3.55 us: forward_parts(): jnp.einsum('wba,wbz->baz', slice_weights, point_features, precision=lax.P...]
    all_to_all x0 -> x1, blocking collectives: none -> 13.1 us  [sum_all(): lax.all_to_all(jnp.broadcast_to(part[None], (32, 9, 1, 128)), PLANE, 0, 0)]
    pallas_call x0 -> x2, Pallas kernels: none -> 9.87 us  [the longest x1 8.18 us: per_device(): pl.pallas_call(back_kernel, out_shape=(jax.ShapeDtypeStruct((rows, width)...]
    all_to_all x1 -> x0, waiting for transfers between devices: 7.24 us -> none  [sum_all(): lax.all_to_all(jnp.broadcast_to(part[None], (32, 9, 1, 128)), PLANE, 0, 0)]
    all_to_all x1 -> x0, starting transfers between devices: 5.59 us -> none  [sum_all(): lax.all_to_all(jnp.broadcast_to(part[None], (32, 9, 1, 128)), PLANE, 0, 0)]
    unnamed x74 -> x30, local copies, waits for them, and re-layouts: 9.25 us -> 5.35 us
    reduce_sum x6 -> x0, other arithmetic: 2.49 us -> none  [the longest x1 1.16 us: forward_parts(): mean = jnp.mean(xf, -1, keepdims=True)]
    div x7 -> x0, other arithmetic: 1.61 us -> none  [the longest x1 0.61 us: forward_parts(): jax.nn.softmax(logits / temper[None, :, None], axis=-1)]
  transfers between devices with their start and end apart: 1 -> 0, of which waited for: 1 -> 0; matrix products, arithmetic and copies ran while one was open for 1% -> 0% of each run, Pallas kernels for 0% -> 0%
where the time goes in v2:
time: 73.2 us; the launch traced here: 72.9 us
  blocking collectives  56 us (77%)
  Pallas kernels  9.87 us (13%)
  local copies, waits for them, and re-layouts  5.47 us (7%)
  between operations  1.37 us (2%)
    all_to_all x1, blocking collectives, sum_all(): lax.all_to_all(jnp.broadcast_to(part[None], (16, 9, 1, 128)), 'z', 0, 0)  25.3 us
    all_to_all x1, blocking collectives, sum_all(): part = lax.all_to_all(flat.reshape(32, 9, 1, 128), PLANE, 0, 0).sum(0)  17.6 us
    all_to_all x1, blocking collectives, sum_all(): lax.all_to_all(jnp.broadcast_to(part[None], (32, 9, 1, 128)), PLANE, 0, 0)  13.1 us
    pallas_call x1, Pallas kernels, per_device(): pl.pallas_call(back_kernel, out_shape=(jax.ShapeDtypeStruct((rows, width)...  8.18 us
    unnamed x30, local copies, waits for them, and re-layouts  5.35 us
    pallas_call x1, Pallas kernels, per_device(): pl.pallas_call(front_kernel, out_shape=(jax.ShapeDtypeStruct((288, 128),...  1.69 us

profile of v2, /device:TPU:1, one launch (start us, length us, event | category | flops | bytes accessed | tf_op | source)
XLA Modules:
  0.0 72.9 jit_solution(16950270633340901122)
XLA Ops:
  1.3 0.0 copy-start.13
  1.3 0.0 copy-start.14
  1.3 0.7 copy-done.13
  2.0 0.0 copy-done.14
  2.0 0.0 copy-start
  2.0 0.9 %copy-done = bf16[512,256]{1,0:T(8,128)(2,1)S(1)} copy-done((bf16[512,256]{1,0:T(8,128)(2,1)S(1)}, bf16[512,256]{1,0:T(8,128)(2,1)}, u32[]{:S(2)}) %copy-start) | copy-done | bytes 262168
  2.9 0.0 copy-start.2
  2.9 0.9 %copy-done.2 = bf16[256,512]{1,0:T(8,128)(2,1)S(1)} copy-done((bf16[256,512]{1,0:T(8,128)(2,1)S(1)}, bf16[256,512]{1,0:T(8,128)(2,1)}, u32[]{:S(2)}) %copy-start.2) | copy-done | bytes 262168
  3.9 0.0 copy-start.4
  3.9 0.9 %copy-done.4 = bf16[512,256]{1,0:T(8,128)(2,1)S(1)} copy-done((bf16[512,256]{1,0:T(8,128)(2,1)S(1)}, bf16[512,256]{1,0:T(8,128)(2,1)}, u32[]{:S(2)}) %copy-start.4) | copy-done | bytes 262168
  4.8 0.0 copy-start.6
  4.8 0.9 %copy-done.6 = bf16[256,256]{1,0:T(8,128)(2,1)S(1)} copy-done((bf16[256,256]{1,0:T(8,128)(2,1)S(1)}, bf16[256,256]{1,0:T(8,128)(2,1)}, u32[]{:S(2)}) %copy-start.6) | copy-done | bytes 131096
  5.7 0.0 copy-start.8
  5.7 0.9 %copy-done.8 = bf16[256,256]{1,0:T(8,128)(2,1)S(1)} copy-done((bf16[256,256]{1,0:T(8,128)(2,1)S(1)}, bf16[256,256]{1,0:T(8,128)(2,1)}, u32[]{:S(2)}) %copy-start.8) | copy-done | bytes 131096
  6.6 0.0 copy-start.11
  6.6 1.7 %front.1 = (f32[288,128]{1,0:T(8,128)S(1)}, f32[512,512]{1,0:T(8,128)S(1)}, bf16[512,512]{1,0:T(8,128)(2,1)S(1)}) custom-call(s32[1,1]{1,0:T(1,128)S(6)} %copy.18.count, f32[8]{0:T(128)S(1)} %copy-done.14, bf16[512,256]{1,0:T(8,128)(2,1)S(1)} %copy-done, f32[1,256]{1,0:T(1,128)S(1)} %bitcast.5, bf16[256,256]{1,0:T(8,128)(2,1)S(1)} %copy-done.6, ...), custom_call_target="tpu_custom_call" | custom-call | tf_op jit(solution)/shard_map/front/pallas_call | solution.py:163
  8.3 17.6 %all_to_all.15 = f32[32,9,1,128]{3,2,1,0:T(1,128)S(1)} all-to-all(f32[32,9,1,128]{3,2,1,0:T(1,128)S(1)} %bitcast.4), channel_id=1, replica_groups=mesh['z'=16,'xh'=2,'c'=2,'xl'=2,'y'=4] {'xh','c','xl','y'}, dimensions={0} | all-to-all | bytes 294912 | tf_op jit(solution)/shard_map/all_to_all | solution.py:136
  25.9 0.1 reduce_sum.18
  26.0 0.0 copy-start.7
  26.0 25.3 %all_to_all.16 = f32[16,9,1,128]{3,2,1,0:T(1,128)S(1)} all-to-all(f32[16,9,1,128]{3,2,1,0:T(1,128)S(1)} %broadcast_in_dim.4), channel_id=1, replica_groups=mesh['z'=16,'xh'=2,'c'=2,'xl'=2,'y'=4] {'z'}, dimensions={0} | all-to-all | bytes 147456 | tf_op jit(solution)/shard_map/all_to_all | solution.py:137
  51.4 0.1 reduce_sum.19
  51.4 0.1 broadcast_in_dim.5
  51.5 13.1 %all_to_all.17 = f32[32,9,1,128]{3,2,1,0:T(1,128)S(1)} all-to-all(f32[32,9,1,128]{3,2,1,0:T(1,128)S(1)} %broadcast_in_dim.5), channel_id=1, replica_groups=mesh['z'=16,'xh'=2,'c'=2,'xl'=2,'y'=4] {'xh','c','xl','y'}, dimensions={0} | all-to-all | bytes 294912 | tf_op jit(solution)/shard_map/all_to_all | solution.py:138
  64.6 0.0 copy-done.11
  64.6 0.0 copy-done.12
  64.6 0.0 copy-done.9
  64.6 0.0 copy-done.10
  64.6 0.0 copy-done.5
  64.7 0.0 copy-done.7
  64.7 0.0 copy-done.1
  64.7 0.0 copy-done.3
  64.7 8.2 %back.1 = (bf16[512,256]{1,0:T(8,128)(2,1)}, bf16[512,256]{1,0:T(8,128)(2,1)}) custom-call(f32[8]{0:T(128)S(1)} %copy-done.14, f32[288,128]{1,0:T(8,128)S(1)} %bitcast.3, f32[8,32,32]{2,1,0:T(8,128)S(1)} %copy-done.10, f32[8,32,32]{2,1,0:T(8,128)S(1)} %copy-done.11, f32[8,32,32]{2,1,0:T(8,128)S(1)} %copy-done.12, bf16[512,256]{1,0:T(8,128)(2,1)S(1)} %copy-done.1, ...), custom_call_target="tpu_custom_call" | custom-call | tf_op jit(solution)/shard_map/back/pallas_call | solution.py:177
  (7 shorter events, 0.0 us)
Async XLA Ops:
  1.3 0.7 copy-start.13
  1.3 0.7 copy-start.14
  2.0 1.0 %copy-start = (bf16[512,256]{1,0:T(8,128)(2,1)S(1)}, bf16[512,256]{1,0:T(8,128)(2,1)}, u32[]{:S(2)}) copy-start(bf16[512,256]{1,0:T(8,128)(2,1)} %x_ref.3) | copy-start | bytes 786436
  2.9 0.9 %copy-start.2 = (bf16[256,512]{1,0:T(8,128)(2,1)S(1)}, bf16[256,512]{1,0:T(8,128)(2,1)}, u32[]{:S(2)}) copy-start(bf16[256,512]{1,0:T(8,128)(2,1)} %w_slice.3) | copy-start | bytes 786436
  3.9 0.9 %copy-start.4 = (bf16[512,256]{1,0:T(8,128)(2,1)S(1)}, bf16[512,256]{1,0:T(8,128)(2,1)}, u32[]{:S(2)}) copy-start(bf16[512,256]{1,0:T(8,128)(2,1)} %cot.3) | copy-start | bytes 786436
  4.8 0.9 %copy-start.6 = (bf16[256,256]{1,0:T(8,128)(2,1)S(1)}, bf16[256,256]{1,0:T(8,128)(2,1)}, u32[]{:S(2)}) copy-start(bf16[256,256]{1,0:T(8,128)(2,1)} %w_fx.3) | copy-start | bytes 393220
  5.7 0.9 %copy-start.8 = (bf16[256,256]{1,0:T(8,128)(2,1)S(1)}, bf16[256,256]{1,0:T(8,128)(2,1)}, u32[]{:S(2)}) copy-start(bf16[256,256]{1,0:T(8,128)(2,1)} %w_out.3) | copy-start | bytes 393220
  6.6 58.0 %copy-start.11 = (f32[8,32,32]{2,1,0:T(8,128)S(1)}, f32[8,32,32]{2,1,0:T(8,128)}, u32[]{:S(2)}) copy-start(f32[8,32,32]{2,1,0:T(8,128)} %key.1) | copy-start | bytes 98308
  6.6 58.0 %copy-start.12 = (f32[8,32,32]{2,1,0:T(8,128)S(1)}, f32[8,32,32]{2,1,0:T(8,128)}, u32[]{:S(2)}) copy-start(f32[8,32,32]{2,1,0:T(8,128)} %value.1) | copy-start | bytes 98308
  8.3 56.3 %copy-start.9 = (bf16[256,256]{1,0:T(8,128)(2,1)S(1)}, bf16[256,256]{1,0:T(8,128)(2,1)}, u32[]{:S(2)}) copy-start(bf16[256,256]{1,0:T(8,128)(2,1)} %w_out.3) | copy-start | bytes 393220
  8.3 56.3 %copy-start.10 = (f32[8,32,32]{2,1,0:T(8,128)S(1)}, f32[8,32,32]{2,1,0:T(8,128)}, u32[]{:S(2)}) copy-start(f32[8,32,32]{2,1,0:T(8,128)} %query.1) | copy-start | bytes 98308
  25.9 38.8 %copy-start.5 = (bf16[512,256]{1,0:T(8,128)(2,1)S(1)}, bf16[512,256]{1,0:T(8,128)(2,1)}, u32[]{:S(2)}) copy-start(bf16[512,256]{1,0:T(8,128)(2,1)} %cot.3) | copy-start | bytes 786436
  26.0 38.6 %copy-start.7 = (bf16[256,256]{1,0:T(8,128)(2,1)S(1)}, bf16[256,256]{1,0:T(8,128)(2,1)}, u32[]{:S(2)}) copy-start(bf16[256,256]{1,0:T(8,128)(2,1)} %w_fx.3) | copy-start | bytes 393220
  51.4 13.3 %copy-start.1 = (bf16[512,256]{1,0:T(8,128)(2,1)S(1)}, bf16[512,256]{1,0:T(8,128)(2,1)}, u32[]{:S(2)}) copy-start(bf16[512,256]{1,0:T(8,128)(2,1)} %x_ref.3) | copy-start | bytes 786436
  51.4 13.3 %copy-start.3 = (bf16[256,512]{1,0:T(8,128)(2,1)S(1)}, bf16[256,512]{1,0:T(8,128)(2,1)}, u32[]{:S(2)}) copy-start(bf16[256,512]{1,0:T(8,128)(2,1)} %w_slice.3) | copy-start | bytes 786436

commit v3 on v2

--- a/solution.py
+++ b/solution.py
@@ -20,7 +20,9 @@
 
 
 def exact(a, b, ca, cb):
-    return dot(a, b, ca, cb, lax.Precision.HIGHEST)
+    a_hi, b_hi = a.astype(BF16), b.astype(BF16)
+    a_lo, b_lo = (a - a_hi.astype(F32)).astype(BF16), (b - b_hi.astype(F32)).astype(BF16)
+    return dot(a_hi, b_hi, ca, cb) + (dot(a_lo, b_hi, ca, cb) + dot(a_hi, b_lo, ca, cb))
 
 
 def normalise(x):
@@ -29,11 +31,25 @@
     return cent * rstd, rstd
 
 
-def front_kernel(
-    count, temper, x_ref, gain, w_fx, w_slice, w_out, cot, flat, w_t, c_t, logit_t, w_bf
-):
+def front_kernel(*refs):
+    count, temper_hbm = refs[:2]
+    sources = refs[2:11]
+    flat, w_t, c_t, scales = refs[11:15]
+    targets = refs[15:24]
+    temper, logit_t, w_bf, sems = refs[24:]
+    x_ref, gain, w_slice, w_fx, w_out, cot = targets[:6]
     rows = x_ref.shape[0]
+    copies = [
+        pltpu.make_async_copy(a, b, sems.at[i])
+        for i, (a, b) in enumerate(zip((*sources, temper_hbm), (*targets, temper)))
+    ]
+    for copy in copies:
+        copy.start()
+    copies[0].wait()
+    copies[1].wait()
     normed = (normalise(x_ref[...].astype(F32))[0] * gain[...]).astype(BF16)
+    for copy in copies[2:]:
+        copy.wait()
     logit_t[...] = dot(w_slice[...].T, normed, 1, 1)
     feats = dot(w_fx[...].T, normed, 1, 1).astype(BF16)
     gmix = dot(w_out[...], cot[...], 1, 1).astype(BF16)
@@ -45,6 +61,7 @@
         part = slice(h * SLICES, (h + 1) * SLICES)
         logits = logit_t[part, :]
         scale = 1.0 / jnp.full((1, rows), temper[h], F32)
+        scales[h : h + 1, :] = scale
         e = jnp.exp((logits - jnp.max(logits, 0, keepdims=True)) * scale)
         w = e * (live / jnp.sum(e, 0, keepdims=True))
         w_t[part, :] = w
@@ -66,33 +83,44 @@
         lax.broadcasted_iota(jnp.int32, (128, 128), 0) // 64
         == lax.broadcasted_iota(jnp.int32, (128, 128), 1) // 64
     )
-    for p in range(4):
-        heads = (2 * p, 2 * p + 1)
-        t = flat[p * 64 : (p + 1) * 64, :]
-        rec = 1.0 / (den_cols[:, p : p + 1] + 1e-05)
-        tok = jnp.concatenate([t[:, 0:32], t[:, 64:96]], 0) * rec
-        g_att = jnp.concatenate([t[:, 32:64], t[:, 96:128]], 0)
-
-        def project(a, weights, side):
-            return jnp.concatenate(
-                [exact(a[i * 64 : (i + 1) * 64], weights[h], 1, side) for i, h in enumerate(heads)],
+    pairs = range(4)
+    scale = 1.0 / math.sqrt(DH)
+
+    def project(a, weights, side):
+        return [
+            jnp.concatenate(
+                [exact(a[p][i * 64 : (i + 1) * 64], weights[2 * p + i], 1, side) for i in range(2)],
                 0,
             )
-
-        q, k, v = project(tok, query, 0), project(tok, key, 0), project(tok, value, 0)
-        scale = 1.0 / math.sqrt(DH)
-        s = jnp.where(own, exact(q, k, 1, 1) * scale, -jnp.inf)
-        e = jnp.exp(s - jnp.max(s, -1, keepdims=True))
-        prob = e / jnp.sum(e, -1, keepdims=True)
-        att = exact(prob, v, 1, 0)
-        g_v = exact(prob, g_att, 0, 0)
-        g_prob = exact(g_att, v, 1, 1)
-        g_s = prob * (g_prob - jnp.sum(prob * g_prob, -1, keepdims=True)) * scale
-        g_q, g_k = exact(g_s, k, 1, 0), exact(g_s, q, 0, 0)
-        g_tok = project(g_q, query, 1) + project(g_k, key, 1) + project(g_v, value, 1)
-        g_num = g_tok * rec
-        gden[p * 128 : (p + 1) * 128, :] = -jnp.sum(tok * g_num, -1, keepdims=True)
-        block = jnp.concatenate([g_num, att], 1)
+            for p in pairs
+        ]
+
+    def each(f, *lists):
+        return [f(*items) for items in zip(*lists)]
+
+    t = [flat[p * 64 : (p + 1) * 64, :] for p in pairs]
+    rec = [1.0 / (den_cols[:, p : p + 1] + 1e-05) for p in pairs]
+    tok = each(lambda t, r: jnp.concatenate([t[:, 0:32], t[:, 64:96]], 0) * r, t, rec)
+    g_att = each(lambda t: jnp.concatenate([t[:, 32:64], t[:, 96:128]], 0), t)
+    q, k, v = project(tok, query, 0), project(tok, key, 0), project(tok, value, 0)
+    s = each(lambda q, k: jnp.where(own, exact(q, k, 1, 1) * scale, -jnp.inf), q, k)
+    g_prob = each(lambda g, v: exact(g, v, 1, 1), g_att, v)
+    e = each(lambda s: jnp.exp(s - jnp.max(s, -1, keepdims=True)), s)
+    prob = each(lambda e: e / jnp.sum(e, -1, keepdims=True), e)
+    g_s = each(
+        lambda w, g: w * (g - jnp.sum(w * g, -1, keepdims=True)) * scale, prob, g_prob
+    )
+    att = each(lambda w, v: exact(w, v, 1, 0), prob, v)
+    g_v = each(lambda w, g: exact(w, g, 0, 0), prob, g_att)
+    g_q = each(lambda g, k: exact(g, k, 1, 0), g_s, k)
+    g_k = each(lambda g, q: exact(g, q, 0, 0), g_s, q)
+    g_tok = each(
+        lambda a, b, c: a + b + c, project(g_q, query, 1), project(g_k, key, 1), project(g_v, value, 1)
+    )
+    for p in pairs:
+        g_num = g_tok[p] * rec[p]
+        gden[p * 128 : (p + 1) * 128, :] = -jnp.sum(tok[p] * g_num, -1, keepdims=True)
+        block = jnp.concatenate([g_num, att[p]], 1)
         block = jnp.where(own, jnp.concatenate([block, block], 1), 0.0)
         hi = block.astype(BF16)
         b_hi[p * 128 : (p + 1) * 128, :] = hi
@@ -100,10 +128,9 @@
 
 
 def back_kernel(
-    temper, flat, query, key, value, x_ref, gain, w_fx, w_slice, w_out, cot, w_t, c_t,
+    flat, w_t, c_t, scales, x_ref, gain, w_slice, w_fx, w_out, cot, query, key, value,
     updated, grad, b_hi, b_lo, gden, g_logit, g_feat, mixed_t,
 ):
-    rows = x_ref.shape[0]
     middle(flat, query, key, value, b_hi, b_lo, gden)
     for p in range(4):
         part = slice(p * 128, (p + 1) * 128)
@@ -116,7 +143,7 @@
             g_feat[h * 32 : (h + 1) * 32, :] = both[i * 64 : i * 64 + 32].astype(BF16)
             mixed_t[h * 32 : (h + 1) * 32, :] = both[i * 64 + 32 : i * 64 + 64]
             mine = slice(i * 64, (i + 1) * 64)
-            scale = 1.0 / jnp.full((1, rows), temper[h], F32)
+            scale = scales[h : h + 1, :]
             wh, gh = w[mine], g_w[mine]
             mean = jnp.sum(wh * gh, 0, keepdims=True)
             g_logit[h * 64 : (h + 1) * 64, :] = (wh * (gh - mean) * scale).astype(BF16)
@@ -141,6 +168,7 @@
 
 VMEM = pl.BlockSpec(memory_space=pltpu.VMEM)
 SMEM = pl.BlockSpec(memory_space=pltpu.SMEM)
+HBM = pl.BlockSpec(memory_space=pltpu.HBM)
 PARAMS = pltpu.CompilerParams(vmem_limit_bytes=32 * 1024 * 1024)
 
 
@@ -160,24 +188,34 @@
     rows, width = points.shape
     gain = norm_gain.reshape(1, width)
     n = HEADS * SLICES
-    flat, w_t, c_t = pl.pallas_call(
+    kept = (
+        points, gain, w_slice, w_fx, w_out, cotangent, query_projection, key_projection,
+        value_projection,
+    )
+    flat, *rest = pl.pallas_call(
         front_kernel,
         out_shape=(
             jax.ShapeDtypeStruct((288, 128), F32),
             jax.ShapeDtypeStruct((n, rows), F32),
             jax.ShapeDtypeStruct((n, rows), BF16),
+            jax.ShapeDtypeStruct((HEADS, rows), F32),
+            *(jax.ShapeDtypeStruct(a.shape, a.dtype) for a in kept),
         ),
-        in_specs=[SMEM] * 2 + [VMEM] * 6,
-        out_specs=(VMEM,) * 3,
-        scratch_shapes=[pltpu.VMEM((n, rows), F32), pltpu.VMEM((n, rows), BF16)],
+        in_specs=[SMEM] + [HBM] * 10,
+        out_specs=(VMEM,) * 13,
+        scratch_shapes=[
+            pltpu.SMEM((HEADS,), F32),
+            pltpu.VMEM((n, rows), F32),
+            pltpu.VMEM((n, rows), BF16),
+            pltpu.SemaphoreType.DMA((10,)),
+        ],
         compiler_params=PARAMS,
         name="front",
-    )(counts, temper, points, gain, w_fx, w_slice, w_out, cotangent)
-    flat = sum_all(flat)
+    )(counts, *(pltpu.with_memory_space_constraint(a, pltpu.HBM) for a in (temper, *kept)))
     return pl.pallas_call(
         back_kernel,
         out_shape=(jax.ShapeDtypeStruct((rows, width), BF16),) * 2,
-        in_specs=[SMEM] + [VMEM] * 12,
+        in_specs=[VMEM] * 13,
         out_specs=(VMEM,) * 2,
         scratch_shapes=[
             pltpu.VMEM((n, 128), BF16),
@@ -189,10 +227,7 @@
         ],
         compiler_params=PARAMS,
         name="back",
-    )(
-        temper, flat, query_projection, key_projection, value_projection, points, gain, w_fx,
-        w_slice, w_out, cotangent, w_t, c_t,
-    )
+    )(sum_all(flat), *rest)
 
 
 def solution(mesh):

time: 73.2 us -> 64 us (0.87)
  local copies, waits for them, and re-layouts: 5.47 us -> 0.12 us
  Pallas kernels: 9.87 us -> 6.47 us
    unnamed x30 -> x0, local copies, waits for them, and re-layouts: 5.35 us -> none
    pallas_call x1, Pallas kernels: 8.18 us -> 4.09 us  [per_device(): pl.pallas_call(back_kernel, out_shape=(jax.ShapeDtypeStruct((rows, width)...]
where the time goes in v3:
time: 64 us; the launch traced here: 63.8 us
  blocking collectives  55.7 us (87%)
  Pallas kernels  6.47 us (10%)
  between operations  1.31 us (2%)
    all_to_all x1, blocking collectives, sum_all(): lax.all_to_all(jnp.broadcast_to(part[None], (16, 9, 1, 128)), 'z', 0, 0)  25.2 us
    all_to_all x1, blocking collectives, sum_all(): part = lax.all_to_all(flat.reshape(32, 9, 1, 128), PLANE, 0, 0).sum(0)  17.4 us
    all_to_all x1, blocking collectives, sum_all(): lax.all_to_all(jnp.broadcast_to(part[None], (32, 9, 1, 128)), PLANE, 0, 0)  13.1 us
    pallas_call x1, Pallas kernels, per_device(): pl.pallas_call(back_kernel, out_shape=(jax.ShapeDtypeStruct((rows, width)...  4.09 us
    pallas_call x1, Pallas kernels, per_device(): pl.pallas_call(front_kernel, out_shape=(jax.ShapeDtypeStruct((288, 128),...  2.38 us

profile of v3, /device:TPU:1, one launch (start us, length us, event | category | flops | bytes accessed | tf_op | source)
XLA Modules:
  0.0 63.8 jit_solution(8246994990890814553)
XLA Ops:
  1.3 2.4 %front.1 = (f32[288,128]{1,0:T(8,128)S(1)}, f32[512,512]{1,0:T(8,128)S(1)}, bf16[512,512]{1,0:T(8,128)(2,1)S(1)}, f32[8,512]{1,0:T(8,128)S(1)}, bf16[512,256]{1,...) custom-call(s32[1,1]{1,0:T(1,128)S(6)} %copy.18.refs_0_, ...), custom_call_target="tpu_custom_call" | custom-call | tf_op jit(solution)/shard_map/front/pallas_call | solution.py:195
  3.7 17.4 %all_to_all.15 = f32[32,9,1,128]{3,2,1,0:T(1,128)S(1)} all-to-all(f32[32,9,1,128]{3,2,1,0:T(1,128)S(1)} %bitcast.4), channel_id=1, replica_groups=mesh['z'=16,'xh'=2,'c'=2,'xl'=2,'y'=4] {'xh','c','xl','y'}, dimensions={0} | all-to-all | bytes 294912 | tf_op jit(solution)/shard_map/all_to_all | solution.py:163
  21.1 0.1 reduce_sum.18
  21.2 25.2 %all_to_all.16 = f32[16,9,1,128]{3,2,1,0:T(1,128)S(1)} all-to-all(f32[16,9,1,128]{3,2,1,0:T(1,128)S(1)} %broadcast_in_dim.4), channel_id=1, replica_groups=mesh['z'=16,'xh'=2,'c'=2,'xl'=2,'y'=4] {'z'}, dimensions={0} | all-to-all | bytes 147456 | tf_op jit(solution)/shard_map/all_to_all | solution.py:164
  46.4 0.1 reduce_sum.19
  46.5 0.1 broadcast_in_dim.5
  46.6 13.1 %all_to_all.17 = f32[32,9,1,128]{3,2,1,0:T(1,128)S(1)} all-to-all(f32[32,9,1,128]{3,2,1,0:T(1,128)S(1)} %broadcast_in_dim.5), channel_id=1, replica_groups=mesh['z'=16,'xh'=2,'c'=2,'xl'=2,'y'=4] {'xh','c','xl','y'}, dimensions={0} | all-to-all | bytes 294912 | tf_op jit(solution)/shard_map/all_to_all | solution.py:165
  59.7 4.1 %back.1 = (bf16[512,256]{1,0:T(8,128)(2,1)}, bf16[512,256]{1,0:T(8,128)(2,1)}) custom-call(f32[288,128]{1,0:T(8,128)S(1)} %bitcast.3, f32[512,512]{1,0:T(8,128)S(1)} %get-tuple-element.16.w_t, bf16[512,512]{1,0:T(8,128)(2,1)S(1)} %get-tuple-element.17.c_t, f32[8,512]{1,0:T(8,128)S(1)} %get-tuple-element.18.scales, ...), custom_call_target="tpu_custom_call" | custom-call | tf_op jit(solution)/shard_map/back/pallas_call | solution.py:215
  (1 shorter events, 0.0 us)

commit v4 on v3

v4 whole, which is shorter than its diff:
```python
import math

import jax
import jax.numpy as jnp
from jax import lax
from jax.experimental import pallas as pl
from jax.experimental.pallas import tpu as pltpu
from jax.sharding import Mesh, PartitionSpec as P

PLANE = ("xh", "c", "xl", "y")
ALL = ("z", "xh", "c", "xl", "y")
HEADS, SLICES, DH = 8, 64, 32
F32, BF16 = jnp.float32, jnp.bfloat16


def dot(a, b, ca, cb, precision=None):
    return lax.dot_general(
        a, b, (((ca,), (cb,)), ((), ())), precision=precision, preferred_element_type=F32
    )


def parts(a):
    hi = a.astype(BF16)
    return hi, (a - hi.astype(F32)).astype(BF16)


def dot3(a, b, ca, cb):
    n = b[0].shape[1 - cb]
    left = jnp.concatenate(a, ca)
    right = jnp.concatenate([jnp.concatenate([b[0], b[0]], cb), jnp.concatenate([b[1], jnp.zeros_like(b[1])], cb)], 1 - cb)
    both = dot(left, right, ca, cb)
    return both[:, :n] + both[:, n:]


def normalise(x):
    cent = x - jnp.mean(x, -1, keepdims=True)
    rstd = lax.rsqrt(jnp.mean(cent * cent, -1, keepdims=True) + 1e-05)
    return cent * rstd, rstd


def front_kernel(*refs):
    count, temper_hbm = refs[:2]
    sources = refs[2:11]
    flat, w_t, w_bf, c_t, scales, w_hi, w_lo = refs[11:18]
    temper, logit_t, sems = refs[27:30]
    targets = refs[18:24] + refs[24:27]
    x_ref, gain, w_slice, w_fx, w_out, cot = targets[:6]
    rows = x_ref.shape[0]
    copies = [
        pltpu.make_async_copy(a, b, sems.at[i])
        for i, (a, b) in enumerate(zip((*sources, temper_hbm), (*targets, temper)))
    ]
    for copy in copies:
        copy.start()
    copies[0].wait()
    copies[1].wait()
    normed = (normalise(x_ref[...].astype(F32))[0] * gain[...]).astype(BF16)
    for copy in copies[2:]:
        copy.wait()
    logit_t[...] = dot(w_slice[...].T, normed, 1, 1)
    stack_weights(*targets[6:], w_hi, w_lo)
    feats = dot(w_fx[...].T, normed, 1, 1).astype(BF16)
    gmix = dot(w_out[...], cot[...], 1, 1).astype(BF16)
    for h in range(HEADS):
        c_t[h * 64 : h * 64 + 32, :] = feats[h * 32 : h * 32 + 32, :]
        c_t[h * 64 + 32 : h * 64 + 64, :] = gmix[h * 32 : h * 32 + 32, :]
    live = (lax.broadcasted_iota(jnp.int32, (1, rows), 1) < count[...]).astype(F32)
    for h in range(HEADS):
        part = slice(h * SLICES, (h + 1) * SLICES)
        logits = logit_t[part, :]
        scale = 1.0 / jnp.full((1, rows), temper[h], F32)
        scales[h : h + 1, :] = scale
        e = jnp.exp((logits - jnp.max(logits, 0, keepdims=True)) * scale)
        w = e * (live / jnp.sum(e, 0, keepdims=True))
        w_t[part, :] = w
        w_bf[part, :] = w.astype(BF16)
    lane = lax.broadcasted_iota(jnp.int32, (64, 128), 1)
    for p in range(4):
        part = slice(p * 128, (p + 1) * 128)
        both = dot(w_bf[part, :], c_t[part, :], 1, 1)
        flat[p * 64 : (p + 1) * 64, :] = jnp.where(lane < 64, both[:64], both[64:])
    den = dot(jnp.ones((8, rows), BF16), w_bf[...], 1, 1)
    flat[256:288, :] = jnp.zeros((32, 128), F32)
    for p in range(4):
        flat[256 + p : 257 + p, :] = den[0:1, p * 128 : (p + 1) * 128]


def stack_weights(query, key, value, hi, lo):
    for h in range(HEADS):
        q, k, v = query[h], key[h], value[h]
        a, a_t, v_t = dot3(parts(q), parts(k), 1, 1), dot3(parts(k), parts(q), 1, 1), v.T
        none, gap = jnp.zeros((32, 32), F32), jnp.zeros((32, 64), F32)

        def at(left, right):
            block = jnp.concatenate([left, right], 1)
            return [block, gap] if h % 2 == 0 else [gap, block]

        upper = jnp.concatenate([*at(a, v), *at(a_t, none), gap, gap], 1)
        lower = jnp.concatenate([gap, gap, gap, gap, *at(v_t, none)], 1)
        whole = jnp.concatenate([upper, lower], 0)
        for ref, part in zip((hi, lo), parts(whole)):
            ref[h * 64 : (h + 1) * 64, :] = part


def middle(flat, w_hi, w_lo):
    row = lax.broadcasted_iota(jnp.int32, (128, 128), 0)
    lane = lax.broadcasted_iota(jnp.int32, (128, 128), 1)
    own = row // 64 == lane // 64
    second = (lane // 32) % 2 == 1
    scale = 1.0 / math.sqrt(DH)
    pairs = range(4)

    def each(f, *lists):
        return [f(*items) for items in zip(*lists)]

    def part(p):
        return slice(p * 128, (p + 1) * 128)

    t = [flat[p * 64 : (p + 1) * 64, :] for p in pairs]
    t = each(lambda t: jnp.where(own, jnp.concatenate([t, t], 0), 0.0), t)
    num = each(lambda t: jnp.where(second, 0.0, t), t)
    rec = 1.0 / (flat[256:264, :] + 1e-05)
    along = [rec[p : p + 1, :] for p in pairs]
    rec = rec.T
    down = [rec[:, p : p + 1] for p in pairs]
    split = each(parts, t)
    raw = [dot3(split[p], (w_hi[part(p), :], w_lo[part(p), :]), 1, 0) for p in pairs]
    u_v, u_t, g_v = (each(lambda a: parts(a[:, part(i)]), raw) for i in range(3))
    num_split = each(parts, num)
    s = each(
        lambda u, n, a, d: jnp.where(own, dot3(u, n, 1, 1) * (scale * a) * d, -jnp.inf),
        u_v, num_split, along, down,
    )
    g_prob = each(lambda g, n, a: dot3(g, n, 1, 1) * a, g_v, num_split, along)
    e = each(lambda s: jnp.exp(s - jnp.max(s, -1, keepdims=True)), s)
    prob = each(lambda e: e * (1.0 / jnp.sum(e, -1, keepdims=True)), e)
    g_s = each(lambda w, g: w * (g - jnp.sum(w * g, -1, keepdims=True)) * scale, prob, g_prob)
    g_tok = each(
        lambda g, w, u_v, u_t, g_v, a, d: dot3(parts(g * a), u_t, 1, 0)
        + dot3(parts(g * d), u_v, 0, 0)
        + dot3(parts(w), g_v, 0, 0),
        g_s, prob, u_v, u_t, g_v, along, down,
    )
    att = each(lambda w, a, v: dot3(parts(w * a), v, 1, 0), prob, along, u_v)
    blocks = each(lambda a, g, d: jnp.where(second, a, g * d), att, g_tok, down)
    g_den = each(lambda n, b, d: -jnp.sum(n * b, -1, keepdims=True) * d, num, blocks, down)
    return blocks, g_den


def back_kernel(
    flat, w_t, w_bf, c_t, scales, x_ref, gain, w_slice, w_fx, w_out, cot, w_hi, w_lo,
    updated_hbm, grad_hbm, updated, grad, g_logit, g_feat, mixed_t, sems,
):
    blocks, g_den = middle(flat, w_hi, w_lo)
    split = [parts(b) for b in blocks]
    total, width = x_ref.shape
    half = total // 2
    copies = []

    def leave(i, at, source, target):
        copies.append(pltpu.make_async_copy(source.at[at], target.at[at], sems.at[i]))
        copies[-1].start()

    for j in range(2):
        at = slice(j * half, (j + 1) * half)
        for p in range(4):
            part = slice(p * 128, (p + 1) * 128)
            c = c_t[part, at]
            g_w = dot(jnp.concatenate(split[p], 1), jnp.concatenate([c, c], 0), 1, 0) + g_den[p]
            both = dot(split[p][0], w_bf[part, at], 0, 0)
            for i in range(2):
                h = 2 * p + i
                mine = slice(h * SLICES, (h + 1) * SLICES)
                w, g = w_t[mine, at], g_w[i * 64 : (i + 1) * 64]
                mean = jnp.sum(w * g, 0, keepdims=True)
                g_logit[mine, at] = (w * (g - mean) * scales[h : h + 1, at]).astype(BF16)
                g_feat[h * 32 : (h + 1) * 32, at] = both[i * 64 : i * 64 + 32].astype(BF16)
                mixed_t[h * 32 : (h + 1) * 32, at] = both[i * 64 + 32 : i * 64 + 64]
        x = x_ref[at, :].astype(F32)
        mixed = mixed_t[:, at].T.astype(BF16)
        updated[at, :] = (x + dot(mixed, w_out[...], 1, 0)).astype(BF16)
        leave(2 * j, pl.ds(j * half, half), updated, updated_hbm)
        g_normed = dot(w_slice[...], g_logit[:, at], 1, 0) + dot(w_fx[...], g_feat[:, at], 1, 0)
        g_normed = g_normed.T.astype(BF16).astype(F32)
        hat, rstd = normalise(x)
        g_hat = g_normed * gain[...]
        along = jnp.mean(g_hat * hat, -1, keepdims=True)
        g_x = rstd * (g_hat - jnp.mean(g_hat, -1, keepdims=True) - hat * along)
        grad[at, :] = (cot[at, :].astype(F32) + g_x).astype(BF16)
        leave(2 * j + 1, pl.ds(j * half, half), grad, grad_hbm)
    for copy in copies:
        copy.wait()


def sum_all(flat):
    part = lax.all_to_all(flat.reshape(32, 9, 1, 128), PLANE, 0, 0).sum(0)
    part = lax.all_to_all(jnp.broadcast_to(part[None], (16, 9, 1, 128)), "z", 0, 0).sum(0)
    whole = lax.all_to_all(jnp.broadcast_to(part[None], (32, 9, 1, 128)), PLANE, 0, 0)
    return whole.reshape(288, 128)


VMEM = pl.BlockSpec(memory_space=pltpu.VMEM)
HBM = pl.BlockSpec(memory_space=pltpu.HBM)
PARAMS = pltpu.CompilerParams(vmem_limit_bytes=32 * 1024 * 1024)


def per_device(
    points,
    counts,
    norm_gain,
    w_fx,
    w_slice,
    temper,
    query_projection,
    key_projection,
    value_projection,
    w_out,
    cotangent,
):
    rows, width = points.shape
    gain = norm_gain.reshape(1, width)
    n = HEADS * SLICES
    kept = (points, gain, w_slice, w_fx, w_out, cotangent)
    projections = (query_projection, key_projection, value_projection)

    def like(*shapes):
        return tuple(jax.ShapeDtypeStruct(shape, kind) for shape, kind in shapes)

    flat, w_t, w_bf, c_t, scales, w_hi, w_lo, *kept = pl.pallas_call(
        front_kernel,
        out_shape=like(
            ((288, 128), F32),
            ((n, rows), F32),
            ((n, rows), BF16),
            ((n, rows), BF16),
            ((HEADS, rows), F32),
            ((n, 384), BF16),
            ((n, 384), BF16),
            *((a.shape, a.dtype) for a in kept),
        ),
        in_specs=[VMEM] + [HBM] * 10,
        out_specs=(VMEM,) * 13,
        scratch_shapes=[
            *(pltpu.VMEM(a.shape, F32) for a in projections),
            pltpu.SMEM((HEADS,), F32),
            pltpu.VMEM((n, rows), F32),
            pltpu.SemaphoreType.DMA((10,)),
        ],
        compiler_params=PARAMS,
        name="front",
    )(
        counts,
        *(pltpu.with_memory_space_constraint(a, pltpu.HBM) for a in (temper, *kept, *projections)),
    )
    return pl.pallas_call(
        back_kernel,
        out_shape=like(((rows, width), BF16), ((rows, width), BF16)),
        in_specs=[VMEM] * 13,
        out_specs=(HBM,) * 2,
        scratch_shapes=[
            pltpu.VMEM((rows, width), BF16),
            pltpu.VMEM((rows, width), BF16),
            pltpu.VMEM((n, rows), BF16),
            pltpu.VMEM((width, rows), BF16),
            pltpu.VMEM((width, rows), F32),
            pltpu.SemaphoreType.DMA((4,)),
        ],
        compiler_params=PARAMS,
        name="back",
    )(sum_all(flat), w_t, w_bf, c_t, scales, *kept, w_hi, w_lo)


def solution(mesh):
    fine = Mesh(mesh.devices.reshape(16, 2, 2, 2, 4), ALL)
    rows = P(ALL, None)
    return jax.shard_map(
        per_device,
        mesh=fine,
        in_specs=(rows, P(("z", "xh", "c"), ("xl", "y"))) + (P(),) * 8 + (rows,),
        out_specs=(rows, rows),
        check_vma=False,
    )
```

time: 64 us -> 70.9 us (1.11)
  local copies, waits for them, and re-layouts: 0.12 us -> 4.15 us
  other arithmetic: 0.16 us -> 3.14 us
    unnamed x0 -> x12, local copies, waits for them, and re-layouts: none -> 2.59 us
    reduce_sum x1, other arithmetic: 0.1 us -> 1.6 us  [sum_all(): part = lax.all_to_all(flat.reshape(32, 9, 1, 128), PLANE, 0, 0).sum(0)]
    reduce_sum x1, other arithmetic: 0.06 us -> 1.54 us  [sum_all(): lax.all_to_all(jnp.broadcast_to(part[None], (16, 9, 1, 128)), 'z', 0, 0)]
    broadcast_in_dim x1, local copies, waits for them, and re-layouts: 0.08 us -> 0.82 us  [sum_all(): jnp.broadcast_to(part[None], (32, 9, 1, 128))]
where the time goes in v4:
time: 70.9 us; the launch traced here: 70.5 us
  blocking collectives  56.1 us (79%)
  Pallas kernels  5.88 us (8%)
  local copies, waits for them, and re-layouts  4.15 us (6%)
  other arithmetic  3.14 us (4%)
  between operations  1.32 us (2%)
    all_to_all x1, blocking collectives, sum_all(): lax.all_to_all(jnp.broadcast_to(part[None], (16, 9, 1, 128)), 'z', 0, 0)  24.7 us
    all_to_all x1, blocking collectives, sum_all(): part = lax.all_to_all(flat.reshape(32, 9, 1, 128), PLANE, 0, 0).sum(0)  18.1 us
    all_to_all x1, blocking collectives, sum_all(): lax.all_to_all(jnp.broadcast_to(part[None], (32, 9, 1, 128)), PLANE, 0, 0)  13.2 us
    pallas_call x1, Pallas kernels, per_device(): pl.pallas_call(back_kernel, out_shape=like(((rows, width), BF16), ((rows,...  3.2 us
    pallas_call x1, Pallas kernels, per_device(): pl.pallas_call(front_kernel, out_shape=like(((288, 128), F32), ((n, rows)...  2.68 us
    unnamed x12, local copies, waits for them, and re-layouts  2.59 us
    reduce_sum x1, other arithmetic, sum_all(): part = lax.all_to_all(flat.reshape(32, 9, 1, 128), PLANE, 0, 0).sum(0)  1.6 us
    reduce_sum x1, other arithmetic, sum_all(): lax.all_to_all(jnp.broadcast_to(part[None], (16, 9, 1, 128)), 'z', 0, 0)  1.54 us

profile of v4, /device:TPU:1, one launch (start us, length us, event | category | flops | bytes accessed | tf_op | source)
XLA Modules:
  0.0 70.5 jit_solution(15513886087973176860)
XLA Ops:
  1.3 2.7 %front.1 = (f32[288,128]{1,0:T(8,128)S(1)}, f32[512,512]{1,0:T(8,128)S(1)}, bf16[512,512]{1,0:T(8,128)(2,1)S(1)}, bf16[512,512]{1,0:T(8,128)(2,1)S(1)}, f32[8,51...) custom-call(s32[1,1]{1,0:T(1,128)S(6)} %copy.18.refs_0_, ...), custom_call_target="tpu_custom_call" | custom-call | tf_op jit(solution)/shard_map/front/pallas_call | solution.py:229
  4.0 0.0 copy-start
  4.0 0.7 copy-done
  4.7 0.0 copy-start.2
  4.7 0.7 copy-done.2
  5.3 0.0 copy-start.4
  5.3 0.6 copy-done.4
  5.9 18.1 %all_to_all.15 = f32[32,9,1,128]{3,2,1,0:T(1,128)} all-to-all(f32[32,9,1,128]{3,2,1,0:T(1,128)S(1)} %bitcast.4), channel_id=1, replica_groups=mesh['z'=16,'xh'=2,'c'=2,'xl'=2,'y'=4] {'xh','c','xl','y'}, dimensions={0} | all-to-all | bytes 294912 | tf_op jit(solution)/shard_map/all_to_all | solution.py:196
  24.0 1.6 %reduce_sum.18 = f32[9,128]{1,0:T(8,128)} reduce(f32[32,9,1,128]{3,2,1,0:T(1,128)} %all_to_all.15, f32[]{:T(128)} %constant.0.clone.1), dimensions={0,2}, to_apply=%region_0.0 | reduce | flops 35712 | bytes 152068 | tf_op jit(solution)/shard_map/reduce_sum | solution.py:196
  25.6 0.7 %broadcast_in_dim.4 = f32[16,9,1,128]{3,2,1,0:T(1,128)S(1)} broadcast(f32[9,128]{1,0:T(8,128)} %reduce_sum.18), dimensions={1,3} | broadcast | bytes 78336 | tf_op jit(solution)/shard_map/broadcast_in_dim | solution.py:197
  26.3 24.7 %all_to_all.16 = f32[16,9,1,128]{3,2,1,0:T(1,128)} all-to-all(f32[16,9,1,128]{3,2,1,0:T(1,128)S(1)} %broadcast_in_dim.4), channel_id=1, replica_groups=mesh['z'=16,'xh'=2,'c'=2,'xl'=2,'y'=4] {'z'}, dimensions={0} | all-to-all | bytes 147456 | tf_op jit(solution)/shard_map/all_to_all | solution.py:197
  51.1 1.5 %reduce_sum.19 = f32[9,128]{1,0:T(8,128)} reduce(f32[16,9,1,128]{3,2,1,0:T(1,128)} %all_to_all.16, f32[]{:T(128)} %constant.0.clone.1), dimensions={0,2}, to_apply=%region_1.0 | reduce | flops 17280 | bytes 78340 | tf_op jit(solution)/shard_map/reduce_sum | solution.py:197
  52.6 0.0 copy-start.1
  52.6 0.8 %broadcast_in_dim.5 = f32[32,9,1,128]{3,2,1,0:T(1,128)S(1)} broadcast(f32[9,128]{1,0:T(8,128)} %reduce_sum.19), dimensions={1,3} | broadcast | bytes 152064 | tf_op jit(solution)/shard_map/broadcast_in_dim | solution.py:198
  53.4 0.0 copy-start.3
  53.4 13.2 %all_to_all.17 = f32[32,9,1,128]{3,2,1,0:T(1,128)S(1)} all-to-all(f32[32,9,1,128]{3,2,1,0:T(1,128)S(1)} %broadcast_in_dim.5), channel_id=1, replica_groups=mesh['z'=16,'xh'=2,'c'=2,'xl'=2,'y'=4] {'xh','c','xl','y'}, dimensions={0} | all-to-all | bytes 294912 | tf_op jit(solution)/shard_map/all_to_all | solution.py:198
  66.7 0.0 copy-start.5
  66.7 0.0 copy-done.1
  66.7 0.0 copy-done.3
  66.7 0.7 copy-done.5
  67.3 3.2 %back.1 = (bf16[512,256]{1,0:T(8,128)(2,1)}, bf16[512,256]{1,0:T(8,128)(2,1)}) custom-call(f32[288,128]{1,0:T(8,128)S(1)} %bitcast.3, f32[512,512]{1,0:T(8,128)S(1)} %get-tuple-element.16.w_t, bf16[512,512]{1,0:T(8,128)(2,1)S(1)} %get-tuple-element.17.w_bf, bf16[512,512]{1,0:T(8,128)(2,1)S(1)} %get-tuple-element.18.c_t, ...), custom_call_target="tpu_custom_call" | custom-call | tf_op jit(solution)/shard_map/back/pallas_call | solution.py:255
Async XLA Ops:
  4.0 0.7 copy-start
  4.7 0.7 copy-start.2
  5.3 0.6 copy-start.4
  52.6 14.1 %copy-start.1 = (bf16[512,256]{1,0:T(8,128)(2,1)S(1)}, bf16[512,256]{1,0:T(8,128)(2,1)}, u32[]{:S(2)}) copy-start(bf16[512,256]{1,0:T(8,128)(2,1)} %copy-done) | copy-start | bytes 786436
  53.4 13.2 %copy-start.3 = (bf16[256,256]{1,0:T(8,128)(2,1)S(1)}, bf16[256,256]{1,0:T(8,128)(2,1)}, u32[]{:S(2)}) copy-start(bf16[256,256]{1,0:T(8,128)(2,1)} %copy-done.2) | copy-start | bytes 393220
  66.7 0.7 copy-start.5

commit v5 on v4

--- a/solution.py
+++ b/solution.py
@@ -10,6 +10,8 @@
 PLANE = ("xh", "c", "xl", "y")
 ALL = ("z", "xh", "c", "xl", "y")
 HEADS, SLICES, DH = 8, 64, 32
+Z_ORDER = [8, 9, 10, 11, 12, 13, 14, 15, 0, 1, 2, 3, 4, 5, 6, 7]
+PLANE_ORDER = [18, 0, 1, 2, 3, 4, 5, 6, 7, 8, 9, 10, 11, 12, 13, 14, 15, 16, 17, 19, 20, 21, 22, 23, 24, 25, 26, 27, 28, 29, 30, 31]
 F32, BF16 = jnp.float32, jnp.bfloat16
 
 
@@ -41,7 +43,7 @@
 def front_kernel(*refs):
     count, temper_hbm = refs[:2]
     sources = refs[2:11]
-    flat, w_t, w_bf, c_t, scales, w_hi, w_lo = refs[11:18]
+    flat, whole, w_bf, c_t, scales, w_hi, w_lo = refs[11:18]
     temper, logit_t, sems = refs[27:30]
     targets = refs[18:24] + refs[24:27]
     x_ref, gain, w_slice, w_fx, w_out, cot = targets[:6]
@@ -72,8 +74,9 @@
         scales[h : h + 1, :] = scale
         e = jnp.exp((logits - jnp.max(logits, 0, keepdims=True)) * scale)
         w = e * (live / jnp.sum(e, 0, keepdims=True))
-        w_t[part, :] = w
-        w_bf[part, :] = w.astype(BF16)
+        w = w.astype(BF16)
+        w_bf[part, :] = w
+        whole[h : h + 1, :] = 1.0 / jnp.maximum(jnp.sum(w.astype(F32), 0, keepdims=True), 0.5)
     lane = lax.broadcasted_iota(jnp.int32, (64, 128), 1)
     for p in range(4):
         part = slice(p * 128, (p + 1) * 128)
@@ -148,7 +151,7 @@
 
 
 def back_kernel(
-    flat, w_t, w_bf, c_t, scales, x_ref, gain, w_slice, w_fx, w_out, cot, w_hi, w_lo,
+    flat, whole, w_bf, c_t, scales, x_ref, gain, w_slice, w_fx, w_out, cot, w_hi, w_lo,
     updated_hbm, grad_hbm, updated, grad, g_logit, g_feat, mixed_t, sems,
 ):
     blocks, g_den = middle(flat, w_hi, w_lo)
@@ -171,8 +174,8 @@
             for i in range(2):
                 h = 2 * p + i
                 mine = slice(h * SLICES, (h + 1) * SLICES)
-                w, g = w_t[mine, at], g_w[i * 64 : (i + 1) * 64]
-                mean = jnp.sum(w * g, 0, keepdims=True)
+                w, g = w_bf[mine, at].astype(F32), g_w[i * 64 : (i + 1) * 64]
+                mean = jnp.sum(w * g, 0, keepdims=True) * whole[h : h + 1, at]
                 g_logit[mine, at] = (w * (g - mean) * scales[h : h + 1, at]).astype(BF16)
                 g_feat[h * 32 : (h + 1) * 32, at] = both[i * 64 : i * 64 + 32].astype(BF16)
                 mixed_t[h * 32 : (h + 1) * 32, at] = both[i * 64 + 32 : i * 64 + 64]
@@ -193,9 +196,12 @@
 
 
 def sum_all(flat):
-    part = lax.all_to_all(flat.reshape(32, 9, 1, 128), PLANE, 0, 0).sum(0)
-    part = lax.all_to_all(jnp.broadcast_to(part[None], (16, 9, 1, 128)), "z", 0, 0).sum(0)
-    whole = lax.all_to_all(jnp.broadcast_to(part[None], (32, 9, 1, 128)), PLANE, 0, 0)
+    def trade(parts, axis, order):
+        return lax.all_to_all(parts, axis, 0, 0, axis_index_groups=[order])
+
+    part = trade(flat.reshape(32, 9, 1, 128), PLANE, PLANE_ORDER).sum(0)
+    part = trade(jnp.broadcast_to(part[None], (16, 9, 1, 128)), "z", Z_ORDER).sum(0)
+    whole = trade(jnp.broadcast_to(part[None], (32, 9, 1, 128)), PLANE, PLANE_ORDER)
     return whole.reshape(288, 128)
 
 
@@ -226,11 +232,11 @@
     def like(*shapes):
         return tuple(jax.ShapeDtypeStruct(shape, kind) for shape, kind in shapes)
 
-    flat, w_t, w_bf, c_t, scales, w_hi, w_lo, *kept = pl.pallas_call(
+    flat, whole, w_bf, c_t, scales, w_hi, w_lo, *kept = pl.pallas_call(
         front_kernel,
         out_shape=like(
             ((288, 128), F32),
-            ((n, rows), F32),
+            ((HEADS, rows), F32),
             ((n, rows), BF16),
             ((n, rows), BF16),
             ((HEADS, rows), F32),
@@ -267,7 +273,7 @@
         ],
         compiler_params=PARAMS,
         name="back",
-    )(sum_all(flat), w_t, w_bf, c_t, scales, *kept, w_hi, w_lo)
+    )(sum_all(flat), whole, w_bf, c_t, scales, *kept, w_hi, w_lo)
 
 
 def solution(mesh):

time: 70.9 us -> 55 us (0.78)
  blocking collectives: 56.1 us -> 47.2 us
  local copies, waits for them, and re-layouts: 4.15 us -> 0.12 us
  other arithmetic: 3.14 us -> 0.16 us
    all_to_all x3, blocking collectives: 56.1 us -> 47.2 us  [trade(): return lax.all_to_all(parts, axis, 0, 0, axis_index_groups=[order])]
    reduce_sum x2, other arithmetic: 3.14 us -> 0.16 us  [the longest x1 0.1 us: sum_all(): part = trade(flat.reshape(32, 9, 1, 128), PLANE, PLANE_ORDER).sum(0)]
    unnamed x12 -> x0, local copies, waits for them, and re-layouts: 2.59 us -> none
    broadcast_in_dim x1, local copies, waits for them, and re-layouts: 0.82 us -> 0.08 us  [sum_all(): jnp.broadcast_to(part[None], (32, 9, 1, 128))]
where the time goes in v5:
time: 55 us; the launch traced here: 54.7 us
  blocking collectives  47.2 us (86%)
  Pallas kernels  5.93 us (11%)
  between operations  1.31 us (2%)
    all_to_all x3, blocking collectives, trade(): return lax.all_to_all(parts, axis, 0, 0, axis_index_groups=[order])  47.2 us
    pallas_call x1, Pallas kernels, per_device(): pl.pallas_call(back_kernel, out_shape=like(((rows, width), BF16), ((rows,...  3.27 us
    pallas_call x1, Pallas kernels, per_device(): pl.pallas_call(front_kernel, out_shape=like(((288, 128), F32), ((HEADS, r...  2.67 us

profile of v5, /device:TPU:1, one launch (start us, length us, event | category | flops | bytes accessed | tf_op | source)
XLA Modules:
  0.0 54.7 jit_solution(8147022978430979476)
XLA Ops:
  1.3 2.7 %front.1 = (f32[288,128]{1,0:T(8,128)S(1)}, f32[8,512]{1,0:T(8,128)S(1)}, bf16[512,512]{1,0:T(8,128)(2,1)S(1)}, bf16[512,512]{1,0:T(8,128)(2,1)S(1)}, f32[8,512]...) custom-call(s32[1,1]{1,0:T(1,128)S(6)} %copy.18.refs_0_, ...), custom_call_target="tpu_custom_call" | custom-call | tf_op jit(solution)/shard_map/front/pallas_call | solution.py:235
  4.0 16.8 %all_to_all.15 = f32[32,9,1,128]{3,2,1,0:T(1,128)S(1)} all-to-all(f32[32,9,1,128]{3,2,1,0:T(1,128)S(1)} %bitcast.4), channel_id=1, replica_groups={{18,0,1,2,3,4,5,6,7,8,9,10,11,12,13,14,15,16,17,19,20,21,22,23,24,25,26..., dimensions={0} | all-to-all | bytes 294912 | tf_op jit(solution)/shard_map/all_to_all | solution.py:200
  20.8 0.1 reduce_sum.18
  20.9 18.6 %all_to_all.16 = f32[16,9,1,128]{3,2,1,0:T(1,128)S(1)} all-to-all(f32[16,9,1,128]{3,2,1,0:T(1,128)S(1)} %broadcast_in_dim.4), channel_id=1, replica_groups={{256,288,320,352,384,416,448,480,0,32,64,96,128,160,192,224},{257,289,3..., dimensions={0} | all-to-all | bytes 147456 | tf_op jit(solution)/shard_map/all_to_all | solution.py:200
  39.6 0.1 reduce_sum.19
  39.6 0.1 broadcast_in_dim.5
  39.7 11.8 %all_to_all.17 = f32[32,9,1,128]{3,2,1,0:T(1,128)S(1)} all-to-all(f32[32,9,1,128]{3,2,1,0:T(1,128)S(1)} %broadcast_in_dim.5), channel_id=1, replica_groups={{18,0,1,2,3,4,5,6,7,8,9,10,11,12,13,14,15,16,17,19,20,21,22,23,24,25,26..., dimensions={0} | all-to-all | bytes 294912 | tf_op jit(solution)/shard_map/all_to_all | solution.py:200
  51.5 3.3 %back.1 = (bf16[512,256]{1,0:T(8,128)(2,1)}, bf16[512,256]{1,0:T(8,128)(2,1)}) custom-call(f32[288,128]{1,0:T(8,128)S(1)} %bitcast.3, f32[8,512]{1,0:T(8,128)S(1)} %get-tuple-element.16.whole, bf16[512,512]{1,0:T(8,128)(2,1)S(1)} %get-tuple-element.17.w_bf, bf16[512,512]{1,0:T(8,128)(2,1)S(1)} %get-tuple-element.18.c_t, ...), custom_call_target="tpu_custom_call" | custom-call | tf_op jit(solution)/shard_map/back/pallas_call | solution.py:261
  (1 shorter events, 0.0 us)

commit v6 on v5

--- a/solution.py
+++ b/solution.py
@@ -10,8 +10,8 @@
 PLANE = ("xh", "c", "xl", "y")
 ALL = ("z", "xh", "c", "xl", "y")
 HEADS, SLICES, DH = 8, 64, 32
-Z_ORDER = [8, 9, 10, 11, 12, 13, 14, 15, 0, 1, 2, 3, 4, 5, 6, 7]
-PLANE_ORDER = [18, 0, 1, 2, 3, 4, 5, 6, 7, 8, 9, 10, 11, 12, 13, 14, 15, 16, 17, 19, 20, 21, 22, 23, 24, 25, 26, 27, 28, 29, 30, 31]
+Z_ORDER = [8, 9, 7, 10, 6, 11, 5, 12, 4, 13, 3, 14, 2, 15, 1, 0]
+PLANE_ORDER = [26, *range(26), *range(27, 32)]
 F32, BF16 = jnp.float32, jnp.bfloat16
 
 

time: 55 us -> 53.8 us (0.978)
  blocking collectives: 47.2 us -> 46.1 us
    all_to_all x3, blocking collectives: 47.2 us -> 46.1 us  [trade(): return lax.all_to_all(parts, axis, 0, 0, axis_index_groups=[order])]
where the time goes in v6:
time: 53.8 us; the launch traced here: 53.6 us
  blocking collectives  46.1 us (86%)
  Pallas kernels  5.93 us (11%)
  between operations  1.31 us (2%)
    all_to_all x3, blocking collectives, trade(): return lax.all_to_all(parts, axis, 0, 0, axis_index_groups=[order])  46.1 us
    pallas_call x1, Pallas kernels, per_device(): pl.pallas_call(back_kernel, out_shape=like(((rows, width), BF16), ((rows,...  3.26 us
    pallas_call x1, Pallas kernels, per_device(): pl.pallas_call(front_kernel, out_shape=like(((288, 128), F32), ((HEADS, r...  2.67 us

profile of v6, /device:TPU:1, one launch (start us, length us, event | category | flops | bytes accessed | tf_op | source)
XLA Modules:
  0.0 53.6 jit_solution(14984588568476041479)
XLA Ops:
  1.3 2.7 %front.1 = (f32[288,128]{1,0:T(8,128)S(1)}, f32[8,512]{1,0:T(8,128)S(1)}, bf16[512,512]{1,0:T(8,128)(2,1)S(1)}, bf16[512,512]{1,0:T(8,128)(2,1)S(1)}, f32[8,512]...) custom-call(s32[1,1]{1,0:T(1,128)S(6)} %copy.18.refs_0_, ...), custom_call_target="tpu_custom_call" | custom-call | tf_op jit(solution)/shard_map/front/pallas_call | solution.py:235
  4.0 16.4 %all_to_all.15 = f32[32,9,1,128]{3,2,1,0:T(1,128)S(1)} all-to-all(f32[32,9,1,128]{3,2,1,0:T(1,128)S(1)} %bitcast.4), channel_id=1, replica_groups={{26,0,1,2,3,4,5,6,7,8,9,10,11,12,13,14,15,16,17,18,19,20,21,22,23,24,25..., dimensions={0} | all-to-all | bytes 294912 | tf_op jit(solution)/shard_map/all_to_all | solution.py:200
  20.4 0.1 reduce_sum.18
  20.5 17.9 %all_to_all.16 = f32[16,9,1,128]{3,2,1,0:T(1,128)S(1)} all-to-all(f32[16,9,1,128]{3,2,1,0:T(1,128)S(1)} %broadcast_in_dim.4), channel_id=1, replica_groups={{256,288,224,320,192,352,160,384,128,416,96,448,64,480,32,0},{257,289,2..., dimensions={0} | all-to-all | bytes 147456 | tf_op jit(solution)/shard_map/all_to_all | solution.py:200
  38.4 0.1 reduce_sum.19
  38.5 0.1 broadcast_in_dim.5
  38.6 11.8 %all_to_all.17 = f32[32,9,1,128]{3,2,1,0:T(1,128)S(1)} all-to-all(f32[32,9,1,128]{3,2,1,0:T(1,128)S(1)} %broadcast_in_dim.5), channel_id=1, replica_groups={{26,0,1,2,3,4,5,6,7,8,9,10,11,12,13,14,15,16,17,18,19,20,21,22,23,24,25..., dimensions={0} | all-to-all | bytes 294912 | tf_op jit(solution)/shard_map/all_to_all | solution.py:200
  50.3 3.3 %back.1 = (bf16[512,256]{1,0:T(8,128)(2,1)}, bf16[512,256]{1,0:T(8,128)(2,1)}) custom-call(f32[288,128]{1,0:T(8,128)S(1)} %bitcast.3, f32[8,512]{1,0:T(8,128)S(1)} %get-tuple-element.16.whole, bf16[512,512]{1,0:T(8,128)(2,1)S(1)} %get-tuple-element.17.w_bf, bf16[512,512]{1,0:T(8,128)(2,1)S(1)} %get-tuple-element.18.c_t, ...), custom_call_target="tpu_custom_call" | custom-call | tf_op jit(solution)/shard_map/back/pallas_call | solution.py:261
  (1 shorter events, 0.0 us)

commit v7 on v6

--- a/solution.py
+++ b/solution.py
@@ -82,7 +82,8 @@
         part = slice(p * 128, (p + 1) * 128)
         both = dot(w_bf[part, :], c_t[part, :], 1, 1)
         flat[p * 64 : (p + 1) * 64, :] = jnp.where(lane < 64, both[:64], both[64:])
-    den = dot(jnp.ones((8, rows), BF16), w_bf[...], 1, 1)
+    den = jnp.sum(w_bf[...].astype(F32), 1, keepdims=True)
+    den = jnp.broadcast_to(den, (den.shape[0], 128)).T
     flat[256:288, :] = jnp.zeros((32, 128), F32)
     for p in range(4):
         flat[256 + p : 257 + p, :] = den[0:1, p * 128 : (p + 1) * 128]

time: 53.8 us -> 53.7 us (level)
  no operation moved by 1% of the time
where the time goes in v7:
time: 53.7 us; the launch traced here: 53.4 us
  blocking collectives  46.1 us (86%)
  Pallas kernels  5.78 us (11%)
  between operations  1.31 us (2%)
    all_to_all x3, blocking collectives, trade(): return lax.all_to_all(parts, axis, 0, 0, axis_index_groups=[order])  46.1 us
    pallas_call x1, Pallas kernels, per_device(): pl.pallas_call(back_kernel, out_shape=like(((rows, width), BF16), ((rows,...  3.26 us
    pallas_call x1, Pallas kernels, per_device(): pl.pallas_call(front_kernel, out_shape=like(((288, 128), F32), ((HEADS, r...  2.52 us

profile of v7, /device:TPU:1, one launch (start us, length us, event | category | flops | bytes accessed | tf_op | source)
XLA Modules:
  0.0 53.4 jit_solution(13656151741760376494)
XLA Ops:
  1.3 2.5 %front.1 = (f32[288,128]{1,0:T(8,128)S(1)}, f32[8,512]{1,0:T(8,128)S(1)}, bf16[512,512]{1,0:T(8,128)(2,1)S(1)}, bf16[512,512]{1,0:T(8,128)(2,1)S(1)}, f32[8,512]...) custom-call(s32[1,1]{1,0:T(1,128)S(6)} %copy.18.refs_0_, ...), custom_call_target="tpu_custom_call" | custom-call | tf_op jit(solution)/shard_map/front/pallas_call | solution.py:236
  3.8 16.4 %all_to_all.15 = f32[32,9,1,128]{3,2,1,0:T(1,128)S(1)} all-to-all(f32[32,9,1,128]{3,2,1,0:T(1,128)S(1)} %bitcast.4), channel_id=1, replica_groups={{26,0,1,2,3,4,5,6,7,8,9,10,11,12,13,14,15,16,17,18,19,20,21,22,23,24,25..., dimensions={0} | all-to-all | bytes 294912 | tf_op jit(solution)/shard_map/all_to_all | solution.py:201
  20.2 0.1 reduce_sum.18
  20.4 17.9 %all_to_all.16 = f32[16,9,1,128]{3,2,1,0:T(1,128)S(1)} all-to-all(f32[16,9,1,128]{3,2,1,0:T(1,128)S(1)} %broadcast_in_dim.4), channel_id=1, replica_groups={{256,288,224,320,192,352,160,384,128,416,96,448,64,480,32,0},{257,289,2..., dimensions={0} | all-to-all | bytes 147456 | tf_op jit(solution)/shard_map/all_to_all | solution.py:201
  38.3 0.1 reduce_sum.19
  38.3 0.1 broadcast_in_dim.5
  38.4 11.8 %all_to_all.17 = f32[32,9,1,128]{3,2,1,0:T(1,128)S(1)} all-to-all(f32[32,9,1,128]{3,2,1,0:T(1,128)S(1)} %broadcast_in_dim.5), channel_id=1, replica_groups={{26,0,1,2,3,4,5,6,7,8,9,10,11,12,13,14,15,16,17,18,19,20,21,22,23,24,25..., dimensions={0} | all-to-all | bytes 294912 | tf_op jit(solution)/shard_map/all_to_all | solution.py:201
  50.2 3.3 %back.1 = (bf16[512,256]{1,0:T(8,128)(2,1)}, bf16[512,256]{1,0:T(8,128)(2,1)}) custom-call(f32[288,128]{1,0:T(8,128)S(1)} %bitcast.3, f32[8,512]{1,0:T(8,128)S(1)} %get-tuple-element.16.whole, bf16[512,512]{1,0:T(8,128)(2,1)S(1)} %get-tuple-element.17.w_bf, bf16[512,512]{1,0:T(8,128)(2,1)S(1)} %get-tuple-element.18.c_t, ...), custom_call_target="tpu_custom_call" | custom-call | tf_op jit(solution)/shard_map/back/pallas_call | solution.py:262
  (1 shorter events, 0.0 us)

commit v8 on v7

--- a/solution.py
+++ b/solution.py
@@ -11,7 +11,7 @@
 ALL = ("z", "xh", "c", "xl", "y")
 HEADS, SLICES, DH = 8, 64, 32
 Z_ORDER = [8, 9, 7, 10, 6, 11, 5, 12, 4, 13, 3, 14, 2, 15, 1, 0]
-PLANE_ORDER = [26, *range(26), *range(27, 32)]
+PLANE_ORDER = [26, 18, *(i for i in range(32) if i not in (26, 18, 8)), 8]
 F32, BF16 = jnp.float32, jnp.bfloat16
 
 
@@ -155,6 +155,7 @@
     flat, whole, w_bf, c_t, scales, x_ref, gain, w_slice, w_fx, w_out, cot, w_hi, w_lo,
     updated_hbm, grad_hbm, updated, grad, g_logit, g_feat, mixed_t, sems,
 ):
+    hats = [normalise(x_ref[j * 256 : (j + 1) * 256, :].astype(F32)) for j in range(2)]
     blocks, g_den = middle(flat, w_hi, w_lo)
     split = [parts(b) for b in blocks]
     total, width = x_ref.shape
@@ -186,7 +187,7 @@
         leave(2 * j, pl.ds(j * half, half), updated, updated_hbm)
         g_normed = dot(w_slice[...], g_logit[:, at], 1, 0) + dot(w_fx[...], g_feat[:, at], 1, 0)
         g_normed = g_normed.T.astype(BF16).astype(F32)
-        hat, rstd = normalise(x)
+        hat, rstd = hats[j]
         g_hat = g_normed * gain[...]
         along = jnp.mean(g_hat * hat, -1, keepdims=True)
         g_x = rstd * (g_hat - jnp.mean(g_hat, -1, keepdims=True) - hat * along)

time: 53.7 us -> 53.6 us (level)
  no operation moved by 1% of the time
where the time goes in v8:
time: 53.6 us; the launch traced here: 53.4 us
  blocking collectives  46 us (86%)
  Pallas kernels  5.78 us (11%)
  between operations  1.31 us (2%)
    all_to_all x3, blocking collectives, trade(): return lax.all_to_all(parts, axis, 0, 0, axis_index_groups=[order])  46 us
    pallas_call x1, Pallas kernels, per_device(): pl.pallas_call(back_kernel, out_shape=like(((rows, width), BF16), ((rows,...  3.26 us
    pallas_call x1, Pallas kernels, per_device(): pl.pallas_call(front_kernel, out_shape=like(((288, 128), F32), ((HEADS, r...  2.52 us

profile of v8, /device:TPU:1, one launch (start us, length us, event | category | flops | bytes accessed | tf_op | source)
XLA Modules:
  0.0 53.4 jit_solution(4670233570174765917)
XLA Ops:
  1.3 2.5 %front.1 = (f32[288,128]{1,0:T(8,128)S(1)}, f32[8,512]{1,0:T(8,128)S(1)}, bf16[512,512]{1,0:T(8,128)(2,1)S(1)}, bf16[512,512]{1,0:T(8,128)(2,1)S(1)}, f32[8,512]...) custom-call(s32[1,1]{1,0:T(1,128)S(6)} %copy.18.refs_0_, ...), custom_call_target="tpu_custom_call" | custom-call | tf_op jit(solution)/shard_map/front/pallas_call | solution.py:237
  3.8 16.4 %all_to_all.15 = f32[32,9,1,128]{3,2,1,0:T(1,128)S(1)} all-to-all(f32[32,9,1,128]{3,2,1,0:T(1,128)S(1)} %bitcast.4), channel_id=1, replica_groups={{26,18,0,1,2,3,4,5,6,7,9,10,11,12,13,14,15,16,17,19,20,21,22,23,24,25,2..., dimensions={0} | all-to-all | bytes 294912 | tf_op jit(solution)/shard_map/all_to_all | solution.py:202
  20.2 0.1 reduce_sum.18
  20.3 18.2 %all_to_all.16 = f32[16,9,1,128]{3,2,1,0:T(1,128)S(1)} all-to-all(f32[16,9,1,128]{3,2,1,0:T(1,128)S(1)} %broadcast_in_dim.4), channel_id=1, replica_groups={{256,288,224,320,192,352,160,384,128,416,96,448,64,480,32,0},{257,289,2..., dimensions={0} | all-to-all | bytes 147456 | tf_op jit(solution)/shard_map/all_to_all | solution.py:202
  38.5 0.1 reduce_sum.19
  38.6 0.1 broadcast_in_dim.5
  38.7 11.4 %all_to_all.17 = f32[32,9,1,128]{3,2,1,0:T(1,128)S(1)} all-to-all(f32[32,9,1,128]{3,2,1,0:T(1,128)S(1)} %broadcast_in_dim.5), channel_id=1, replica_groups={{26,18,0,1,2,3,4,5,6,7,9,10,11,12,13,14,15,16,17,19,20,21,22,23,24,25,2..., dimensions={0} | all-to-all | bytes 294912 | tf_op jit(solution)/shard_map/all_to_all | solution.py:202
  50.1 3.3 %back.1 = (bf16[512,256]{1,0:T(8,128)(2,1)}, bf16[512,256]{1,0:T(8,128)(2,1)}) custom-call(f32[288,128]{1,0:T(8,128)S(1)} %bitcast.3, f32[8,512]{1,0:T(8,128)S(1)} %get-tuple-element.16.whole, bf16[512,512]{1,0:T(8,128)(2,1)S(1)} %get-tuple-element.17.w_bf, bf16[512,512]{1,0:T(8,128)(2,1)S(1)} %get-tuple-element.18.c_t, ...), custom_call_target="tpu_custom_call" | custom-call | tf_op jit(solution)/shard_map/back/pallas_call | solution.py:263
  (1 shorter events, 0.0 us)

commit v9 on v8

--- a/solution.py
+++ b/solution.py
@@ -10,7 +10,7 @@
 PLANE = ("xh", "c", "xl", "y")
 ALL = ("z", "xh", "c", "xl", "y")
 HEADS, SLICES, DH = 8, 64, 32
-Z_ORDER = [8, 9, 7, 10, 6, 11, 5, 12, 4, 13, 3, 14, 2, 15, 1, 0]
+Z_ORDER = [9, 8, 10, 7, 11, 6, 12, 5, 13, 4, 14, 3, 15, 2, 1, 0]
 PLANE_ORDER = [26, 18, *(i for i in range(32) if i not in (26, 18, 8)), 8]
 F32, BF16 = jnp.float32, jnp.bfloat16
 

time: 53.6 us -> 53.8 us (level)
  no operation moved by 1% of the time
where the time goes in v9:
time: 53.8 us; the launch traced here: 53.5 us
  blocking collectives  46.2 us (86%)
  Pallas kernels  5.78 us (11%)
  between operations  1.31 us (2%)
    all_to_all x3, blocking collectives, trade(): return lax.all_to_all(parts, axis, 0, 0, axis_index_groups=[order])  46.2 us
    pallas_call x1, Pallas kernels, per_device(): pl.pallas_call(back_kernel, out_shape=like(((rows, width), BF16), ((rows,...  3.27 us
    pallas_call x1, Pallas kernels, per_device(): pl.pallas_call(front_kernel, out_shape=like(((288, 128), F32), ((HEADS, r...  2.52 us

profile of v9, /device:TPU:1, one launch (start us, length us, event | category | flops | bytes accessed | tf_op | source)
XLA Modules:
  0.0 53.5 jit_solution(16350233698010169686)
XLA Ops:
  1.3 2.5 %front.1 = (f32[288,128]{1,0:T(8,128)S(1)}, f32[8,512]{1,0:T(8,128)S(1)}, bf16[512,512]{1,0:T(8,128)(2,1)S(1)}, bf16[512,512]{1,0:T(8,128)(2,1)S(1)}, f32[8,512]...) custom-call(s32[1,1]{1,0:T(1,128)S(6)} %copy.18.refs_0_, ...), custom_call_target="tpu_custom_call" | custom-call | tf_op jit(solution)/shard_map/front/pallas_call | solution.py:237
  3.8 16.4 %all_to_all.15 = f32[32,9,1,128]{3,2,1,0:T(1,128)S(1)} all-to-all(f32[32,9,1,128]{3,2,1,0:T(1,128)S(1)} %bitcast.4), channel_id=1, replica_groups={{26,18,0,1,2,3,4,5,6,7,9,10,11,12,13,14,15,16,17,19,20,21,22,23,24,25,2..., dimensions={0} | all-to-all | bytes 294912 | tf_op jit(solution)/shard_map/all_to_all | solution.py:202
  20.2 0.1 reduce_sum.18
  20.3 17.7 %all_to_all.16 = f32[16,9,1,128]{3,2,1,0:T(1,128)S(1)} all-to-all(f32[16,9,1,128]{3,2,1,0:T(1,128)S(1)} %broadcast_in_dim.4), channel_id=1, replica_groups={{288,256,320,224,352,192,384,160,416,128,448,96,480,64,32,0},{289,257,3..., dimensions={0} | all-to-all | bytes 147456 | tf_op jit(solution)/shard_map/all_to_all | solution.py:202
  38.1 0.1 reduce_sum.19
  38.1 0.1 broadcast_in_dim.5
  38.2 12.1 %all_to_all.17 = f32[32,9,1,128]{3,2,1,0:T(1,128)S(1)} all-to-all(f32[32,9,1,128]{3,2,1,0:T(1,128)S(1)} %broadcast_in_dim.5), channel_id=1, replica_groups={{26,18,0,1,2,3,4,5,6,7,9,10,11,12,13,14,15,16,17,19,20,21,22,23,24,25,2..., dimensions={0} | all-to-all | bytes 294912 | tf_op jit(solution)/shard_map/all_to_all | solution.py:202
  50.3 3.3 %back.1 = (bf16[512,256]{1,0:T(8,128)(2,1)}, bf16[512,256]{1,0:T(8,128)(2,1)}) custom-call(f32[288,128]{1,0:T(8,128)S(1)} %bitcast.3, f32[8,512]{1,0:T(8,128)S(1)} %get-tuple-element.16.whole, bf16[512,512]{1,0:T(8,128)(2,1)S(1)} %get-tuple-element.17.w_bf, bf16[512,512]{1,0:T(8,128)(2,1)S(1)} %get-tuple-element.18.c_t, ...), custom_call_target="tpu_custom_call" | custom-call | tf_op jit(solution)/shard_map/back/pallas_call | solution.py:263
  (1 shorter events, 0.0 us)
